TPU v7x, 512 devices: a whole 4x8x8 slice. The times are simulated.
512 devices in a mesh: slab: 128 (over z_lo, x, y), cross: 4 (over z_hi, core).
Axes of the slice: x: 4, y: 8, z: 8 (z_hi: 2, z_lo: 4; z = z_hi * 4 + z_lo), core: 2. Of those that a mesh axis runs over, the one named last changes fastest.
Arguments:
- populations: float32 [19, 512, 32, 128], P(None, 'slab', 'cross'), may hold values from 0 to 1, as said below
- fluid_mask: int32 [512, 32, 128], P('slab', 'cross'), may hold values 0 or 1
- relaxation: float32 [512, 32, 128], P('slab', 'cross'), may hold values from 0.8 to 1.7
- positions: int32 [3, 2048, 642], P(None, 'slab'), may hold values from -1 to 512, as said below
- triangles: int32 [3, 1280], replicated, may hold values from 0 to 641, as said below
- tension: float32 [2048, 1280], P('slab'), may hold values from 0.0003 to 0.003
- coarse_moments: float32 [4, 65536], P(None, 'slab'), may hold values from -0.2 to 1.2, as said below
- interface: int32 [3, 65536], P(None, ('slab', 'cross')), may hold values from -1 to 65535, as said below
Outputs:
- populations_next: float32 [19, 512, 32, 128], P(None, 'slab', 'cross')
- flow: float32 [3, 512, 32, 128], P(None, 'slab', 'cross')
Inputs may be any that keep to these rules, and one draw needn't show every extreme that they name: `positions`: nodes of membrane m lie in planes 4 * (m // 16) - 1 to 4 * (m // 16) + 4, columns 0 to 31 and rows 0 to 127. `triangles`: each triangle names three different nodes of a membrane. `interface`: in each block of 128 columns (one device's, slab major), row 0 names different cells of that device's block, numbered (plane * 8 + column) * 128 + row, or -1 for an unused slot; rows 1 and 2 name coarse cells. `populations`: populations are positive. `coarse_moments`: row 0 is a positive density, rows 1 to 3 a velocity.
All inputs are finite; a program needn't handle non-finite values. No bound on the sum of `fluid_mask` on one device may be relied on, other than what follows from the above.
Results may differ from a plain program's by a relative error of at most 0.0001.
Values sent between devices are 32-bit elements; how exact they have to be, the bound alone decides.
No kernel may reach another device: no remote copies, remote signals or barrier semaphores. Data moves between devices by JAX's collectives and lax.ppermute only.
A program may use at most 128 MiB of HBM per device.

v0:
```python
import math

import jax
import jax.numpy as jnp
from jax import lax
from jax.experimental import pallas as pl
from jax.experimental.pallas import tpu as pltpu
from jax.sharding import PartitionSpec as P

F32 = jnp.float32
BF16 = jnp.bfloat16
I32 = jnp.int32
ROOT_THREE = math.sqrt(3.0)
VELOCITIES = [
    (0, 0, 0),
    (1, 0, 0),
    (-1, 0, 0),
    (0, 1, 0),
    (0, -1, 0),
    (0, 0, 1),
    (0, 0, -1),
    (1, 1, 0),
    (-1, -1, 0),
    (1, -1, 0),
    (-1, 1, 0),
    (1, 0, 1),
    (-1, 0, -1),
    (1, 0, -1),
    (-1, 0, 1),
    (0, 1, 1),
    (0, -1, -1),
    (0, 1, -1),
    (0, -1, 1),
]
STEPS = 4
PLANES = 4
COLUMNS = 8
ROWS = 128
DEEP = PLANES + 2 * STEPS
WIDE = COLUMNS + 2 * STEPS
CROSS = 4
GROUP = 32
MASKS = (4, 16, 2, 1, 8)
NODES = 768
MEMBRANES = 16
VMEM_LIMIT = 56 * 1024 * 1024


def call(body, outs, scratch=(), flops=0, **more):
    return pl.pallas_call(
        body,
        out_shape=outs,
        scratch_shapes=list(scratch),
        compiler_params=pltpu.CompilerParams(vmem_limit_bytes=VMEM_LIMIT),
        cost_estimate=pl.CostEstimate(flops=flops, bytes_accessed=1 << 20, transcendentals=0),
        **more,
    )


def struct(*shape, dtype=F32):
    return jax.ShapeDtypeStruct(shape, dtype)


def pack_kernel(pops, relax, mask, iface, coarse, own_o, right_o, left_o, iface_o, coarse_o):
    def put(field, z, value):
        own_o[field * 4 + z] = value
        low = (z % 2) * 4
        right_o[field * 2 + z // 2, low : low + 4] = value[4:8]
        left_o[field * 2 + z // 2, low : low + 4] = value[0:4]

    for z in range(PLANES):
        for q in range(19):
            put(q, z, pops[q, z])
        put(19, z, relax[z])
        put(20, z, mask[z].astype(F32))
    tile = jnp.zeros((8, ROWS), F32)
    iface_o[...] = tile
    iface_o[0:3] = iface[...].astype(F32)
    right_o[42] = iface_o[...]
    left_o[42] = iface_o[...]
    for sub in range(4):
        for mom in range(4):
            coarse_o[sub : sub + 1, mom * 128 : (mom + 1) * 128] = coarse[
                mom : mom + 1, sub * 128 : (sub + 1) * 128
            ]


def halo_kernel(from_left, from_right, iface_far, iface_own, halo_o):
    k = lax.axis_index("cross")
    has_right = jnp.where(k < CROSS - 1, 1.0, 0.0).astype(F32)
    has_left = jnp.where(k > 0, 1.0, 0.0).astype(F32)
    for tile in range(42):
        right = from_right[tile] * has_right
        left = from_left[tile] * has_left
        halo_o[2 * tile, 0:4] = right[0:4]
        halo_o[2 * tile + 1, 0:4] = right[4:8]
        halo_o[2 * tile, 4:8] = left[0:4]
        halo_o[2 * tile + 1, 4:8] = left[4:8]
    halo_o[84 + k] = iface_own[...]
    halo_o[84 + (k + 1) % 4] = from_right[42]
    halo_o[84 + (k + 3) % 4] = from_left[42]
    halo_o[84 + (k + 2) % 4] = iface_far[...]


def nodal_kernel(positions, triangles, tension, out, x_s, table_s):
    j = lax.axis_index("slab")
    k = lax.axis_index("cross")
    x_s[...] = jnp.zeros_like(x_s)
    for d in range(3):
        coords = positions[d].astype(F32)
        x_s[d * 16 : d * 16 + 16, 0:642] = coords - coords[:, 0:1]
    tri = triangles[...]
    for low in range(0, NODES, 128):
        ids = lax.broadcasted_iota(I32, (128, 1280), 0) + low
        hit = (ids == tri[0:1]) | (ids == tri[1:2]) | (ids == tri[2:3])
        table_s[low : low + 128] = jnp.where(hit, 1.0, 0.0).astype(BF16)
    x = x_s[...]
    table = table_s[...]
    corners = jnp.dot(x.astype(BF16), table, preferred_element_type=F32)
    s = tension[...]
    weighted = jnp.concatenate([corners[d * 16 : d * 16 + 16] * s for d in range(3)] + [s], axis=0)
    high = weighted.astype(BF16)
    rest = weighted - high.astype(F32)
    middle = rest.astype(BF16)
    low_part = (rest - middle.astype(F32)).astype(BF16)
    stacked = jnp.concatenate([high, middle, low_part], axis=0)
    sums = lax.dot_general(stacked, table, (((1,), (1,)), ((), ())), preferred_element_type=F32)
    total = sums[0:64] + sums[64:128] + sums[128:192]
    out[...] = jnp.zeros_like(out)
    base = (j * PLANES, k * COLUMNS, 0)
    for d in range(3):
        force = total[d * 16 : d * 16 + 16] - 3.0 * x[d * 16 : d * 16 + 16] * total[48:64]
        place = (positions[d] - base[d]).astype(F32)
        for m in range(MEMBRANES):
            out[m, d : d + 1] = force[m : m + 1]
            out[m, 3 + d : 4 + d, 0:642] = place[m : m + 1]


def spread_body(nodes, initial, finished):
    plane_ids = lax.broadcasted_iota(I32, (8, NODES), 0).astype(F32) - 2.0
    column_ids = lax.broadcasted_iota(I32, (WIDE, NODES), 0)
    column_ids = jnp.where(column_ids < 12, column_ids, column_ids - 16).astype(F32)
    row_ids = (lax.broadcasted_iota(I32, (ROWS, NODES), 0).astype(F32) * 0.25).astype(BF16)

    def add(m, running):
        node = nodes[m]
        along_plane = jnp.maximum(0.5 - 0.25 * jnp.abs(plane_ids - node[3:4]), 0.0)
        along_column = jnp.maximum(0.5 - 0.25 * jnp.abs(column_ids - node[4:5]), 0.0)
        row = jnp.broadcast_to(node[5:6] * 0.25, (16, NODES)).astype(BF16)
        row = jnp.concatenate([row] * 8, axis=0)
        along_row = jnp.abs(jnp.abs(row_ids - row) - BF16(16.0))
        along_row = jnp.maximum(along_row - BF16(15.5), BF16(0.0))
        parts = []
        rest = []
        for d in range(3):
            high = node[d : d + 1].astype(BF16).astype(F32)
            parts.append((high * along_column).astype(BF16))
            rest.append(((node[d : d + 1] - high).astype(BF16).astype(F32) * along_column).astype(BF16))
        block = jnp.concatenate(parts + rest, axis=0)
        stacked = []
        for p in range(8):
            weight = jnp.broadcast_to(along_plane[p : p + 1], (16, NODES)).astype(BF16)
            stacked.append(block * jnp.concatenate([weight] * 6, axis=0))
        lhs = jnp.concatenate(stacked, axis=0)
        return running + lax.dot_general(
            lhs, along_row, (((1,), (1,)), ((), ())), preferred_element_type=F32
        )

    return lax.fori_loop(0, nodes.shape[0], add, initial)


def spread_first_kernel(nodes, out):
    out[...] = spread_body(nodes, jnp.zeros((768, ROWS), F32), None)


def spread_last_kernel(nodes, partial, own_o, up_o, down_o, up2_o, down2_o):
    total = spread_body(nodes, partial[...], None)
    for p in range(8):
        for d in range(3):
            low = p * 96 + d * 16
            value = total[low : low + 16] + total[low + 48 : low + 64]
            own_o[p, d] = value
            if p >= 2:
                up_o[p - 2, d] = value
            if p < 6:
                down_o[p, d] = value
            if p >= 6:
                up2_o[p - 6, d] = value
            if p < 2:
                down2_o[p, d] = value


def lookup_kernel(first, second, up, own, down, out):
    k = lax.axis_index("cross")
    place = lax.rem(lax.axis_index("slab"), GROUP)
    table = jnp.concatenate([first[...], second[...]], axis=0).T
    high = table.astype(BF16)
    low = (table - high.astype(F32)).astype(BF16)
    lhs = jnp.concatenate([high, low], axis=1)
    ids = lax.broadcasted_iota(I32, (128, 256), 0)
    for d, source in enumerate((up, own, down)):
        for a in range(CROSS):
            tile = source[a].astype(I32)
            cell = jnp.concatenate([tile[1:2], tile[2:3]], axis=1)
            shard = cell >> 9
            apart = (shard & (GROUP - 1)) ^ place
            block = jnp.zeros_like(cell)
            for bit, mask in enumerate(MASKS):
                block = block + jnp.where((apart & mask) != 0, 1 << bit, 0)
            row = block * 4 + ((cell >> 7) & 3)
            row = jnp.where((shard >> 5) == k, row, -1)
            lane = cell & 127
            hot = jnp.where(ids == row, 1.0, 0.0).astype(BF16)
            found = jnp.dot(
                lhs, jnp.concatenate([hot, hot], axis=0), preferred_element_type=F32
            )
            chosen = ids == lane
            for mom in range(4):
                value = jnp.sum(
                    jnp.where(chosen, found[mom * 128 : mom * 128 + 128], 0.0), axis=0, keepdims=True
                )
                at = (d * CROSS + a) * 4 + mom
                out[at : at + 1] = 0.75 * value[:, 0:128] + 0.25 * value[:, 128:256]


def rolled(value, velocity):
    if velocity[1]:
        value = pltpu.roll(value, velocity[1] % WIDE, 0)
    if velocity[2]:
        value = pltpu.roll(value, velocity[2] % ROWS, 1)
    return value


def moments(fields):
    def pick(d, sign):
        return [f for f, c in zip(fields, VELOCITIES) if c[d] == sign]

    def add(values):
        while len(values) > 1:
            values = [a + b for a, b in zip(values[::2], values[1::2])] + (
                [values[-1]] if len(values) % 2 else []
            )
        return values[0]

    return add(list(fields)), [add(pick(d, 1)) - add(pick(d, -1)) for d in range(3)]


def equilibrium_terms(v):
    base = 1.0 - 1.5 * (v[0] * v[0] + v[1] * v[1] + v[2] * v[2])
    t = [3.0 * x for x in v]
    pairs = []
    for q in range(1, 19, 2):
        c = VELOCITIES[q]
        along = None
        for d in range(3):
            if c[d]:
                term = t[d]
                if along is None:
                    along = term
                else:
                    along = along + term if c[d] == 1 else along - term
        pairs.append((along, base + 0.5 * along * along))
    return base, pairs


def steps_kernel(
    pops, relax, mask, up, down, halo, halo_up, halo_down,
    force, force_m1, force_p1, force_m2, force_p2, v0, v1, v2, v3,
    pops_o, flow_o,
    f_s, g_s, edge_s, hit_s, relax_s, mask_s, force_s, dense_s,
):
    j = lax.axis_index("slab")
    k = lax.axis_index("cross")
    slabs = lax.axis_size("slab")
    for q in range(19):
        span = slice(q * 4, q * 4 + 4)
        f_s[q, 5:9, 0:8] = pops[q]
        f_s[q, 5:9, 8:16] = halo[span]
        f_s[q, 1:5, 0:8] = up[span]
        f_s[q, 1:5, 8:16] = halo_up[span]
        f_s[q, 9:13, 0:8] = down[span]
        f_s[q, 9:13, 8:16] = halo_down[span]
    for field, dest in ((19, relax_s), (20, mask_s)):
        span = slice(field * 4, field * 4 + 4)
        dest[4:8, 0:8] = relax[...] if field == 19 else mask[...].astype(F32)
        dest[4:8, 8:16] = halo[span]
        dest[0:4, 0:8] = up[span]
        dest[0:4, 8:16] = halo_up[span]
        dest[8:12, 0:8] = down[span]
        dest[8:12, 8:16] = halo_down[span]
    for p in range(DEEP):
        inverse = 1.0 / relax_s[p]
        for d in range(3):
            value = None
            for part, low in ((force, 2), (force_m1, 0), (force_p1, 6), (force_m2, 0), (force_p2, 10)):
                if low <= p < low + part.shape[0]:
                    value = part[p - low, d] if value is None else value + part[p - low, d]
            force_s[p, d] = value * inverse

    values = v0[...] + v1[...] + v2[...] + v3[...]
    dense_s[...] = values
    rows64 = lax.broadcasted_iota(I32, (64, 128), 0)
    rows128 = lax.broadcasted_iota(I32, (128, 128), 0)
    ids = lax.broadcasted_iota(I32, (WIDE, ROWS), 0)
    for d, source in enumerate((halo_up, halo, halo_down)):
        slab_there = (j + d - 1 >= 0) & (j + d - 1 < slabs)
        lhs = []
        rhs = []
        for e in (-1, 0, 1):
            member = k + e
            there = slab_there & (member >= 0) & (member < CROSS)
            member = jnp.clip(member, 0, CROSS - 1)
            cell = source[84 + member].astype(I32)[0:1]
            amounts = dense_s[pl.ds(pl.multiple_of((d * CROSS + member) * 4, 4), 4)]
            column = (cell >> 7) & 7
            if e == 0:
                place = column
                fits = cell >= 0
            else:
                place = column + 8
                fits = (cell >= 0) & ((column < 4) if e == 1 else (column >= 4))
            place = jnp.where(fits & there, (cell >> 10) * WIDE + place, -1)
            hot = rows64 == place
            pieces = [jnp.where(hot, 1.0, 0.0).astype(BF16)]
            high = amounts.astype(BF16).astype(F32)
            rest = amounts - high
            middle = rest.astype(BF16).astype(F32)
            last = rest - middle
            for part in (high, middle, last):
                for mom in range(4):
                    pieces.append(jnp.where(hot, part[mom : mom + 1], 0.0).astype(BF16))
            lhs.append(jnp.concatenate(pieces, axis=0))
            rhs.append(jnp.where(rows128 == (cell & 127), 1.0, 0.0).astype(BF16))
        dense = lax.dot_general(
            jnp.concatenate(lhs, axis=1),
            jnp.concatenate(rhs, axis=1),
            (((1,), (1,)), ((), ())),
            preferred_element_type=F32,
        )
        outside_left = (ids >= 12) & (k == 0)
        outside_right = (ids >= 8) & (ids < 12) & (k == CROSS - 1)
        outside = outside_left | outside_right | jnp.logical_not(slab_there)
        for z in range(PLANES):
            p = d * 4 + z
            if p < 1 or p > DEEP - 2:
                continue
            low = z * WIDE

            def taken(mom):
                return (
                    dense[64 * (1 + mom) + low : 64 * (1 + mom) + low + WIDE]
                    + dense[64 * (5 + mom) + low : 64 * (5 + mom) + low + WIDE]
                    + dense[64 * (9 + mom) + low : 64 * (9 + mom) + low + WIDE]
                )

            hit_s[p] = jnp.where(outside, 1.0, dense[low : low + WIDE])
            density = taken(0)
            base, pairs = equilibrium_terms([taken(1), taken(2), taken(3)])
            edge_s[0, p] = density * base * (1.0 / 3.0)
            for n, (along, even) in enumerate(pairs):
                scaled = density * (1.0 / 18.0 if n < 3 else 1.0 / 36.0)
                edge_s[2 * n + 1, p] = scaled * (even + along)
                edge_s[2 * n + 2, p] = scaled * (even - along)

    for step in range(STEPS):
        source, dest = (f_s, g_s) if step % 2 == 0 else (g_s, f_s)

        def plane(p, carry):
            if step == 0:
                fields = [source[q, p + 1] for q in range(19)]
            else:
                hit = hit_s[p] > 0.5
                fields = [jnp.where(hit, edge_s[q, p], source[q, p + 1]) for q in range(19)]
            density, momentum = moments(fields)
            inverse = 1.0 / density
            velocity = [(momentum[d] + force_s[p, d]) * inverse for d in range(3)]
            omega = relax_s[p]
            fluid = mask_s[p] > 0.5
            keep = 1.0 - omega
            amount = omega * density
            base, pairs = equilibrium_terms(velocity)
            dest[0, p + 1] = jnp.where(
                fluid, keep * fields[0] + (amount * (1.0 / 3.0)) * base, fields[0]
            )
            light = amount * (1.0 / 18.0)
            lighter = amount * (1.0 / 36.0)
            for n, (along, even) in enumerate(pairs):
                one, two = fields[2 * n + 1], fields[2 * n + 2]
                scaled = light if n < 3 else lighter
                c = VELOCITIES[2 * n + 1]
                new_one = jnp.where(fluid, keep * one + scaled * (even + along), two)
                new_two = jnp.where(fluid, keep * two + scaled * (even - along), one)
                dest[2 * n + 1, p + 1 + c[0]] = rolled(new_one, c)
                dest[2 * n + 2, p + 1 - c[0]] = rolled(new_two, tuple(-x for x in c))
            return carry

        lax.fori_loop(step, DEEP - step, plane, 0)

    last = f_s if STEPS % 2 == 0 else g_s
    for z in range(PLANES):
        p = STEPS + z
        hit = hit_s[p, 0:8] > 0.5
        fields = [jnp.where(hit, edge_s[q, p, 0:8], last[q, p + 1, 0:8]) for q in range(19)]
        for q in range(19):
            pops_o[q, z] = fields[q]
        density, momentum = moments(fields)
        scale = ROOT_THREE / density
        for d in range(3):
            flow_o[d, z] = momentum[d] * scale


def slab_shift(value, steps):
    count = lax.axis_size("slab")
    pairs = [(s, s + steps) for s in range(count) if 0 <= s + steps < count]
    return lax.ppermute(value, "slab", pairs)


def cross_shift(value, steps):
    return lax.ppermute(value, "cross", [(s, (s + steps) % CROSS) for s in range(CROSS)])


def swap_group_and_cross(value):
    pairs = []
    for group in range(CROSS):
        for place in range(GROUP):
            for k in range(CROSS):
                pairs.append(
                    ((group * GROUP + place) * CROSS + k, (k * GROUP + place) * CROSS + group)
                )
    return lax.ppermute(value, ("slab", "cross"), pairs)


def exchange_masked(value, mask):
    return lax.ppermute(value, "slab", [(s, s ^ mask) for s in range(lax.axis_size("slab"))])


def on_device(
    populations, fluid_mask, relaxation, positions, triangles, tension, coarse_moments, interface
):
    own, to_right, to_left, iface, shard = call(
        pack_kernel,
        (struct(84, 8, ROWS), struct(43, 8, ROWS), struct(43, 8, ROWS), struct(8, ROWS), struct(4, 512)),
    )(populations, relaxation, fluid_mask, interface, coarse_moments)
    table = swap_group_and_cross(shard)
    from_left = cross_shift(to_right, 1)
    from_right = cross_shift(to_left, -1)
    iface_far = cross_shift(iface, 2)
    up = slab_shift(own, 1)
    down = slab_shift(own, -1)
    for mask in MASKS[:-1]:
        table = jnp.concatenate([table, exchange_masked(table, mask)], axis=0)
    other = exchange_masked(table, MASKS[-1])

    halo = call(halo_kernel, struct(88, 8, ROWS))(from_left, from_right, iface_far, iface)
    halo_up = slab_shift(halo, 1)
    halo_down = slab_shift(halo, -1)

    nodes = call(
        nodal_kernel,
        struct(MEMBRANES, 8, NODES),
        [pltpu.VMEM((48, NODES), F32), pltpu.VMEM((NODES, 1280), BF16)],
        flops=1 << 30,
    )(positions, triangles, tension)

    half = MEMBRANES // 2

    def half_spec(at):
        return pl.BlockSpec((half, 8, NODES), lambda i: (at, 0, 0))

    def whole_spec(*shape):
        return pl.BlockSpec(shape, lambda i: (0,) * len(shape))

    partial = call(
        spread_first_kernel,
        struct(768, ROWS),
        grid=(1,),
        in_specs=[half_spec(0)],
        out_specs=whole_spec(768, ROWS),
        flops=1 << 31,
    )(nodes)
    counts = (8, 6, 6, 2, 2)
    force, to_up, to_down, to_up2, to_down2 = call(
        spread_last_kernel,
        tuple(struct(n, 3, WIDE, ROWS) for n in counts),
        grid=(1,),
        in_specs=[half_spec(1), whole_spec(768, ROWS)],
        out_specs=tuple(whole_spec(n, 3, WIDE, ROWS) for n in counts),
        flops=1 << 31,
    )(nodes, partial)
    force_m1 = slab_shift(to_up, 1)
    force_p1 = slab_shift(to_down, -1)
    force_m2 = slab_shift(to_up2, 2)
    force_p2 = slab_shift(to_down2, -2)

    tail = pl.BlockSpec((4, 8, ROWS), lambda i: (21, 0, 0))
    found = call(
        lookup_kernel,
        struct(48, ROWS),
        grid=(1,),
        in_specs=[whole_spec(64, 512), whole_spec(64, 512), tail, tail, tail],
        out_specs=whole_spec(48, ROWS),
        flops=1 << 30,
    )(table, other, halo_up, halo, halo_down)
    found1 = cross_shift(found, 1)
    found2 = cross_shift(found, 2)
    found3 = cross_shift(found, 3)

    state = pltpu.VMEM((19, DEEP + 2, WIDE, ROWS), F32)
    field = pltpu.VMEM((DEEP, WIDE, ROWS), F32)
    return call(
        steps_kernel,
        (struct(*populations.shape), struct(3, *populations.shape[1:])),
        [
            state,
            state,
            pltpu.VMEM((19, DEEP, WIDE, ROWS), F32),
            field,
            field,
            field,
            pltpu.VMEM((DEEP, 3, WIDE, ROWS), F32),
            pltpu.VMEM((48, ROWS), F32),
        ],
        flops=1 << 31,
    )(
        populations, relaxation, fluid_mask, up, down, halo, halo_up, halo_down,
        force, force_m1, force_p1, force_m2, force_p2, found, found1, found2, found3,
    )


def solution(mesh):
    in_specs = (
        P(None, "slab", "cross", None),
        P("slab", "cross", None),
        P("slab", "cross", None),
        P(None, "slab", None),
        P(),
        P("slab", None),
        P(None, "slab"),
        P(None, ("slab", "cross")),
    )
    out_specs = (P(None, "slab", "cross", None), P(None, "slab", "cross", None))
    return jax.shard_map(
        on_device, mesh=mesh, in_specs=in_specs, out_specs=out_specs, check_vma=False
    )
```

profile of v0, /device:TPU:54, one launch (start us, length us, event | category | flops | bytes accessed | tf_op | source)
XLA Modules:
  0.0 135.6 jit_solution(4582839965721379603)
XLA Ops:
  0.6 1.9 %shard_map.95 = (f32[84,8,128]{2,1,0:T(8,128)}, f32[43,8,128]{2,1,0:T(8,128)}, f32[43,8,128]{2,1,0:T(8,128)}, f32[8,128]{1,0:T(8,128)}, f32[4,512]{1,0:T(4,128)}) custom-call(f32[19,4,8,128]{3,2,1,0:T(8,128)} %pops.3, f32[4,8,128]{2,1,0:T(8,128)} %relax.3, s32[4,8,128]{2,1,0:T(8,128)} %mask.3, s32[3,128]{1,0:T(4,128)} %iface.1, f32[4,512]{1,0:T(4,128)} %coarse.1), custom_call_target="tpu_custom_call" | custom-call | bytes 1048576 | tf_op jit(solution)/shard_map/pallas_call | solution.py:440
  2.6 1.3 collective-permute-start.11
  3.9 0.0 collective-permute-done.11
  3.9 3.8 %collective-permute-start.12 = (f32[4,512]{1,0:T(4,128)S(1)}, f32[4,512]{1,0:T(4,128)S(1)}, u32[]{:S(2)}, u32[]{:S(2)}) collective-permute-start(f32[4,512]{1,0:T(4,128)S(1)} %collective-permute-done.11), channel_id=1, source_target_pairs={{0,16},{4,20},{8,24},{12,28},{16,0},{20,4},{24,8},{28,12},{32,48},... | collective-permute-start | bytes 24584 | tf_op jit(solution)/shard_map/ppermute | solution.py:434
  7.7 17.4 %collective-permute-start.4 = (f32[8,128]{1,0:T(8,128)}, f32[8,128]{1,0:T(8,128)S(1)}, u32[]{:S(2)}, u32[]{:S(2)}) collective-permute-start(f32[8,128]{1,0:T(8,128)} %get-tuple-element.15.iface_own), channel_id=1, source_target_pairs={{0,2},{1,3},{2,0},{3,1},{4,6},{5,7},{6,4},{7,5},{8,10},{9,11},{10,... | collective-permute-start | bytes 12296 | tf_op jit(solution)/shard_map/ppermute | solution.py:419
  25.1 1.9 %collective-permute-start.2 = (f32[43,8,128]{2,1,0:T(8,128)}, f32[43,8,128]{2,1,0:T(8,128)S(1)}, u32[]{:S(2)}, u32[]{:S(2)}) collective-permute-start(f32[43,8,128]{2,1,0:T(8,128)} %get-tuple-element.13), channel_id=1, source_target_pairs={{0,1},{1,2},{2,3},{3,0},{4,5},{5,6},{6,7},{7,4},{8,9},{9,10},{10,1... | collective-permute-start | bytes 528392 | tf_op jit(solution)/shard_map/ppermute | solution.py:419
  27.1 7.5 %collective-permute-start.3 = (f32[43,8,128]{2,1,0:T(8,128)}, f32[43,8,128]{2,1,0:T(8,128)S(1)}, u32[]{:S(2)}, u32[]{:S(2)}) collective-permute-start(f32[43,8,128]{2,1,0:T(8,128)} %get-tuple-element.14), channel_id=1, source_target_pairs={{0,3},{1,0},{2,1},{3,2},{4,7},{5,4},{6,5},{7,6},{8,11},{9,8},{10,9... | collective-permute-start | bytes 528392 | tf_op jit(solution)/shard_map/ppermute | solution.py:419
  34.6 0.0 collective-permute-done.12
  34.7 3.3 %collective-permute-start.13 = (f32[8,512]{1,0:T(8,128)S(1)}, f32[8,512]{1,0:T(8,128)S(1)}, u32[]{:S(2)}, u32[]{:S(2)}) collective-permute-start(f32[8,512]{1,0:T(8,128)S(1)} %pad_maximum_fusion.2), channel_id=1, source_target_pairs={{0,64},{4,68},{8,72},{12,76},{16,80},{20,84},{24,88},{28,92},{32,9... | collective-permute-start | bytes 49160 | tf_op jit(solution)/shard_map/ppermute | solution.py:434
  38.0 3.8 %shard_map.97.nodes = f32[16,8,768]{2,1,0:T(8,128)} custom-call(s32[3,16,642]{2,1,0:T(8,128)} %positions.1, s32[3,1280]{1,0:T(4,128)} %triangles.1, f32[16,1280]{1,0:T(8,128)} %tension.1), custom_call_target="tpu_custom_call" | custom-call | flops 1073741824 | bytes 1048576 | tf_op jit(solution)/shard_map/pallas_call | solution.py:458
  41.8 0.0 collective-permute-done.13
  41.8 2.2 %collective-permute-start.14 = (f32[16,512]{1,0:T(8,128)S(1)}, f32[16,512]{1,0:T(8,128)S(1)}, u32[]{:S(2)}, u32[]{:S(2)}) collective-permute-start(f32[16,512]{1,0:T(8,128)S(1)} %pad_maximum_fusion.1), channel_id=1, source_target_pairs={{0,8},{4,12},{8,0},{12,4},{16,24},{20,28},{24,16},{28,20},{32,40},... | collective-permute-start | bytes 98312 | tf_op jit(solution)/shard_map/ppermute | solution.py:434
  44.1 5.8 %shard_map.98.partial = f32[768,128]{1,0:T(8,128)} custom-call(f32[16,8,768]{2,1,0:T(8,128)} %shard_map.97.nodes), custom_call_target="tpu_custom_call" | custom-call | flops 2147483648 | bytes 1048576 | tf_op jit(solution)/shard_map/pallas_call | solution.py:473
  49.9 0.0 collective-permute-done.14
  49.9 3.5 %collective-permute-start.15 = (f32[32,512]{1,0:T(8,128)S(1)}, f32[32,512]{1,0:T(8,128)S(1)}, u32[]{:S(2)}, u32[]{:S(2)}) collective-permute-start(f32[32,512]{1,0:T(8,128)S(1)} %pad_maximum_fusion), channel_id=1, source_target_pairs={{0,4},{4,0},{8,12},{12,8},{16,20},{20,16},{24,28},{28,24},{32,36},... | collective-permute-start | bytes 196616 | tf_op jit(solution)/shard_map/ppermute | solution.py:434
  53.4 0.0 collective-permute-done.4.iface_far
  53.4 0.0 copy-start.3
  53.4 0.0 collective-permute-done.2.from_left
  53.4 0.0 copy-start
  53.5 0.0 collective-permute-done.3.from_right
  53.5 0.6 copy-done.3
  54.0 0.1 copy-done
  54.1 0.7 copy-done.1
  54.8 1.8 %shard_map.96.own.halo = f32[88,8,128]{2,1,0:T(8,128)} custom-call(f32[43,8,128]{2,1,0:T(8,128)} %copy-done, f32[43,8,128]{2,1,0:T(8,128)} %copy-done.1, f32[8,128]{1,0:T(8,128)} %copy-done.3, f32[8,128]{1,0:T(8,128)} %get-tuple-element.15.iface_own), custom_call_target="tpu_custom_call" | custom-call | bytes 1048576 | tf_op jit(solution)/shard_map/pallas_call | solution.py:454
  56.6 3.6 %collective-permute-start.6 = (f32[88,8,128]{2,1,0:T(8,128)}, f32[88,8,128]{2,1,0:T(8,128)S(1)}, u32[]{:S(2)}, u32[]{:S(2)}) collective-permute-start(f32[88,8,128]{2,1,0:T(8,128)} %shard_map.96.own.halo), channel_id=1, source_target_pairs={{4,0},{8,4},{12,8},{16,12},{20,16},{24,20},{28,24},{32,28},{36,32}... | collective-permute-start | bytes 1081352 | tf_op jit(solution)/shard_map/ppermute | solution.py:415
  60.2 2.4 %collective-permute-start.5 = (f32[88,8,128]{2,1,0:T(8,128)}, f32[88,8,128]{2,1,0:T(8,128)S(1)}, u32[]{:S(2)}, u32[]{:S(2)}) collective-permute-start(f32[88,8,128]{2,1,0:T(8,128)} %shard_map.96.own.halo), channel_id=1, source_target_pairs={{0,4},{4,8},{8,12},{12,16},{16,20},{20,24},{24,28},{28,32},{32,36}... | collective-permute-start | bytes 1081352 | tf_op jit(solution)/shard_map/ppermute | solution.py:415
  62.6 6.0 %shard_map.99 = (f32[8,3,16,128]{3,2,1,0:T(8,128)}, f32[6,3,16,128]{3,2,1,0:T(8,128)}, f32[6,3,16,128]{3,2,1,0:T(8,128)}, f32[2,3,16,128]{3,2,1,0:T(8,128)}, f32[2,3,16,128]{3,2,1,0:T(8,128)}) custom-call(f32[16,8,768]{2,1,0:T(8,128)} %shard_map.97.nodes, f32[768,128]{1,0:T(8,128)} %shard_map.98.partial), custom_call_target="tpu_custom_call" | custom-call | flops 2147483648 | bytes 1048576 | tf_op jit(solution)/shard_map/pallas_call | solution.py:482
  68.6 8.1 %collective-permute-start.9 = (f32[2,3,16,128]{3,2,1,0:T(8,128)}, f32[2,3,16,128]{3,2,1,0:T(8,128)S(1)}, u32[]{:S(2)}, u32[]{:S(2)}) collective-permute-start(f32[2,3,16,128]{3,2,1,0:T(8,128)} %get-tuple-element.19), channel_id=1, source_target_pairs={{0,8},{4,12},{8,16},{12,20},{16,24},{20,28},{24,32},{28,36},{32,40... | collective-permute-start | bytes 147464 | tf_op jit(solution)/shard_map/ppermute | solution.py:415
  76.7 2.1 %collective-permute-start.1 = (f32[84,8,128]{2,1,0:T(8,128)S(1)}, f32[84,8,128]{2,1,0:T(8,128)S(1)}, u32[]{:S(2)}, u32[]{:S(2)}) collective-permute-start(f32[84,8,128]{2,1,0:T(8,128)S(1)} %copy-done.6), channel_id=1, source_target_pairs={{4,0},{8,4},{12,8},{16,12},{20,16},{24,20},{28,24},{32,28},{36,32}... | collective-permute-start | bytes 1032200 | tf_op jit(solution)/shard_map/ppermute | solution.py:415
  78.8 0.0 collective-permute-done.15
  78.8 3.9 %collective-permute-start = (f32[84,8,128]{2,1,0:T(8,128)S(1)}, f32[84,8,128]{2,1,0:T(8,128)S(1)}, u32[]{:S(2)}, u32[]{:S(2)}) collective-permute-start(f32[84,8,128]{2,1,0:T(8,128)S(1)} %copy-done.6), channel_id=1, source_target_pairs={{0,4},{4,8},{8,12},{12,16},{16,20},{20,24},{24,28},{28,32},{32,36}... | collective-permute-start | bytes 1032200 | tf_op jit(solution)/shard_map/ppermute | solution.py:415
  82.8 0.0 collective-permute-done.9.force_m2
  82.8 1.9 %collective-permute-start.16 = (f32[64,512]{1,0:T(8,128)S(1)}, f32[64,512]{1,0:T(8,128)S(1)}, u32[]{:S(2)}, u32[]{:S(2)}) collective-permute-start(f32[64,512]{1,0:T(8,128)S(1)} %concatenate.18.first), channel_id=1, source_target_pairs={{0,32},{4,36},{8,40},{12,44},{16,48},{20,52},{24,56},{28,60},{32,0... | collective-permute-start | bytes 393224 | tf_op jit(solution)/shard_map/ppermute | solution.py:434
  84.7 4.9 %collective-permute-done.16.second = f32[64,512]{1,0:T(8,128)S(1)} collective-permute-done((f32[64,512]{1,0:T(8,128)S(1)}, f32[64,512]{1,0:T(8,128)S(1)}, u32[]{:S(2)}, u32[]{:S(2)}) %collective-permute-start.16) | collective-permute-done | bytes 131104 | tf_op jit(solution)/shard_map/ppermute | solution.py:434
  89.7 7.5 %collective-permute-start.7 = (f32[6,3,16,128]{3,2,1,0:T(8,128)}, f32[6,3,16,128]{3,2,1,0:T(8,128)S(1)}, u32[]{:S(2)}, u32[]{:S(2)}) collective-permute-start(f32[6,3,16,128]{3,2,1,0:T(8,128)} %get-tuple-element.17), channel_id=1, source_target_pairs={{0,4},{4,8},{8,12},{12,16},{16,20},{20,24},{24,28},{28,32},{32,36}... | collective-permute-start | bytes 442376 | tf_op jit(solution)/shard_map/ppermute | solution.py:415
  97.1 0.0 collective-permute-done.6.down.halo_down
  97.2 1.9 %collective-permute-start.8 = (f32[6,3,16,128]{3,2,1,0:T(8,128)S(1)}, f32[6,3,16,128]{3,2,1,0:T(8,128)S(1)}, u32[]{:S(2)}, u32[]{:S(2)}) collective-permute-start(f32[6,3,16,128]{3,2,1,0:T(8,128)S(1)} %copy-done.9), channel_id=1, source_target_pairs={{4,0},{8,4},{12,8},{16,12},{20,16},{24,20},{28,24},{32,28},{36,32}... | collective-permute-start | bytes 442376 | tf_op jit(solution)/shard_map/ppermute | solution.py:415
  99.1 0.0 collective-permute-done.5.up.halo_up
  99.1 0.0 copy-start.5
  99.1 0.0 copy-done.14
  99.1 1.9 %collective-permute-start.10 = (f32[2,3,16,128]{3,2,1,0:T(8,128)S(1)}, f32[2,3,16,128]{3,2,1,0:T(8,128)S(1)}, u32[]{:S(2)}, u32[]{:S(2)}) collective-permute-start(f32[2,3,16,128]{3,2,1,0:T(8,128)S(1)} %copy-done.14), channel_id=1, source_target_pairs={{8,0},{12,4},{16,8},{20,12},{24,16},{28,20},{32,24},{36,28},{40,32... | collective-permute-start | bytes 147464 | tf_op jit(solution)/shard_map/ppermute | solution.py:415
  101.0 0.0 copy-done.2
  101.1 0.0 copy-done.12
  101.1 0.0 copy-done.4
  101.1 0.0 copy-done.5
  101.1 3.0 %shard_map.100.v0 = f32[48,128]{1,0:T(8,128)} custom-call(f32[64,512]{1,0:T(8,128)} %copy-done.2, f32[64,512]{1,0:T(8,128)} %copy-done.12, f32[88,8,128]{2,1,0:T(8,128)} %copy-done.5, f32[88,8,128]{2,1,0:T(8,128)} %shard_map.96.own.halo, f32[88,8,128]{2,1,0:T(8,128)} %copy-done.4), custom_call_target="tpu_custom_call" | custom-call | flops 1073741824 | bytes 1048576 | tf_op jit(solution)/shard_map/pallas_call | solution.py:496
  104.1 6.1 %collective-permute-done.10.force_p2 = f32[2,3,16,128]{3,2,1,0:T(8,128)S(1)} collective-permute-done((f32[2,3,16,128]{3,2,1,0:T(8,128)S(1)}, f32[2,3,16,128]{3,2,1,0:T(8,128)S(1)}, u32[]{:S(2)}, u32[]{:S(2)}) %collective-permute-start.10) | collective-permute-done | bytes 49184 | tf_op jit(solution)/shard_map/ppermute | solution.py:415
  110.2 2.1 %collective-permute-start.19 = (f32[48,128]{1,0:T(8,128)}, f32[48,128]{1,0:T(8,128)S(1)}, u32[]{:S(2)}, u32[]{:S(2)}) collective-permute-start(f32[48,128]{1,0:T(8,128)} %shard_map.100.v0), channel_id=1, source_target_pairs={{0,3},{1,0},{2,1},{3,2},{4,7},{5,4},{6,5},{7,6},{8,11},{9,8},{10,9... | collective-permute-start | bytes 73736 | tf_op jit(solution)/shard_map/ppermute | solution.py:419
  112.3 0.0 collective-permute-done.7.force_m1
  112.3 4.3 %collective-permute-start.18 = (f32[48,128]{1,0:T(8,128)}, f32[48,128]{1,0:T(8,128)S(1)}, u32[]{:S(2)}, u32[]{:S(2)}) collective-permute-start(f32[48,128]{1,0:T(8,128)} %shard_map.100.v0), channel_id=1, source_target_pairs={{0,2},{1,3},{2,0},{3,1},{4,6},{5,7},{6,4},{7,5},{8,10},{9,11},{10,... | collective-permute-start | bytes 73736 | tf_op jit(solution)/shard_map/ppermute | solution.py:419
  116.6 0.0 collective-permute-done.8.force_p1
  116.6 0.0 copy-start.11
  116.6 2.1 %collective-permute-start.17 = (f32[48,128]{1,0:T(8,128)}, f32[48,128]{1,0:T(8,128)S(1)}, u32[]{:S(2)}, u32[]{:S(2)}) collective-permute-start(f32[48,128]{1,0:T(8,128)} %shard_map.100.v0), channel_id=1, source_target_pairs={{0,1},{1,2},{2,3},{3,0},{4,5},{5,6},{6,7},{7,4},{8,9},{9,10},{10,1... | collective-permute-start | bytes 73736 | tf_op jit(solution)/shard_map/ppermute | solution.py:419
  118.8 0.0 collective-permute-done.1.down
  118.8 0.0 collective-permute-done.up
  118.8 0.0 collective-permute-done.19.v3
  118.8 3.4 %collective-permute-done.18.v2 = f32[48,128]{1,0:T(8,128)S(1)} collective-permute-done((f32[48,128]{1,0:T(8,128)}, f32[48,128]{1,0:T(8,128)S(1)}, u32[]{:S(2)}, u32[]{:S(2)}) %collective-permute-start.18) | collective-permute-done | bytes 24608 | tf_op jit(solution)/shard_map/ppermute | solution.py:419
  122.2 4.0 %collective-permute-done.17.v1 = f32[48,128]{1,0:T(8,128)S(1)} collective-permute-done((f32[48,128]{1,0:T(8,128)}, f32[48,128]{1,0:T(8,128)S(1)}, u32[]{:S(2)}, u32[]{:S(2)}) %collective-permute-start.17) | collective-permute-done | bytes 24608 | tf_op jit(solution)/shard_map/ppermute | solution.py:419
  126.1 0.0 copy-done.10
  126.2 0.0 copy-done.7
  126.2 0.0 copy-done.8
  126.2 0.0 copy-done.16
  126.2 0.6 copy-done.18
  126.8 8.9 %shard_map.101 = (f32[19,4,8,128]{3,2,1,0:T(8,128)}, f32[3,4,8,128]{3,2,1,0:T(8,128)}) custom-call(f32[19,4,8,128]{3,2,1,0:T(8,128)} %pops.3, f32[4,8,128]{2,1,0:T(8,128)} %relax.3, s32[4,8,128]{2,1,0:T(8,128)} %mask.3, f32[84,8,128]{2,1,0:T(8,128)} %copy-done.8, f32[84,8,128]{2,1,0:T(8,128)} %copy-done.7, f32[88,8,128]{2,1,0:T(8,128)} %shard_map.96.own.halo, ...), custom_call_target="tpu_custom_call" | custom-call | flops 2147483648 | bytes 1048576 | tf_op jit(solution)/shard_map/pallas_call | solution.py:510
  (25 shorter events, 0.1 us)
Async XLA Ops:
  2.6 1.3 collective-permute-start.11
  3.9 30.7 %collective-permute-start.12 = (f32[4,512]{1,0:T(4,128)S(1)}, f32[4,512]{1,0:T(4,128)S(1)}, u32[]{:S(2)}, u32[]{:S(2)}) collective-permute-start(f32[4,512]{1,0:T(4,128)S(1)} %collective-permute-done.11), channel_id=1, source_target_pairs={{0,16},{4,20},{8,24},{12,28},{16,0},{20,4},{24,8},{28,12},{32,48},... | collective-permute-start | bytes 24584 | tf_op jit(solution)/shard_map/ppermute | solution.py:434
  7.7 45.7 %collective-permute-start.4 = (f32[8,128]{1,0:T(8,128)}, f32[8,128]{1,0:T(8,128)S(1)}, u32[]{:S(2)}, u32[]{:S(2)}) collective-permute-start(f32[8,128]{1,0:T(8,128)} %get-tuple-element.15.iface_own), channel_id=1, source_target_pairs={{0,2},{1,3},{2,0},{3,1},{4,6},{5,7},{6,4},{7,5},{8,10},{9,11},{10,... | collective-permute-start | bytes 12296 | tf_op jit(solution)/shard_map/ppermute | solution.py:419
  25.1 28.3 %collective-permute-start.2 = (f32[43,8,128]{2,1,0:T(8,128)}, f32[43,8,128]{2,1,0:T(8,128)S(1)}, u32[]{:S(2)}, u32[]{:S(2)}) collective-permute-start(f32[43,8,128]{2,1,0:T(8,128)} %get-tuple-element.13), channel_id=1, source_target_pairs={{0,1},{1,2},{2,3},{3,0},{4,5},{5,6},{6,7},{7,4},{8,9},{9,10},{10,1... | collective-permute-start | bytes 528392 | tf_op jit(solution)/shard_map/ppermute | solution.py:419
  27.1 26.4 %collective-permute-start.3 = (f32[43,8,128]{2,1,0:T(8,128)}, f32[43,8,128]{2,1,0:T(8,128)S(1)}, u32[]{:S(2)}, u32[]{:S(2)}) collective-permute-start(f32[43,8,128]{2,1,0:T(8,128)} %get-tuple-element.14), channel_id=1, source_target_pairs={{0,3},{1,0},{2,1},{3,2},{4,7},{5,4},{6,5},{7,6},{8,11},{9,8},{10,9... | collective-permute-start | bytes 528392 | tf_op jit(solution)/shard_map/ppermute | solution.py:419
  34.7 7.2 %collective-permute-start.13 = (f32[8,512]{1,0:T(8,128)S(1)}, f32[8,512]{1,0:T(8,128)S(1)}, u32[]{:S(2)}, u32[]{:S(2)}) collective-permute-start(f32[8,512]{1,0:T(8,128)S(1)} %pad_maximum_fusion.2), channel_id=1, source_target_pairs={{0,64},{4,68},{8,72},{12,76},{16,80},{20,84},{24,88},{28,92},{32,9... | collective-permute-start | bytes 49160 | tf_op jit(solution)/shard_map/ppermute | solution.py:434
  41.8 8.1 %collective-permute-start.14 = (f32[16,512]{1,0:T(8,128)S(1)}, f32[16,512]{1,0:T(8,128)S(1)}, u32[]{:S(2)}, u32[]{:S(2)}) collective-permute-start(f32[16,512]{1,0:T(8,128)S(1)} %pad_maximum_fusion.1), channel_id=1, source_target_pairs={{0,8},{4,12},{8,0},{12,4},{16,24},{20,28},{24,16},{28,20},{32,40},... | collective-permute-start | bytes 98312 | tf_op jit(solution)/shard_map/ppermute | solution.py:434
  49.9 28.9 %collective-permute-start.15 = (f32[32,512]{1,0:T(8,128)S(1)}, f32[32,512]{1,0:T(8,128)S(1)}, u32[]{:S(2)}, u32[]{:S(2)}) collective-permute-start(f32[32,512]{1,0:T(8,128)S(1)} %pad_maximum_fusion), channel_id=1, source_target_pairs={{0,4},{4,0},{8,12},{12,8},{16,20},{20,16},{24,28},{28,24},{32,36},... | collective-permute-start | bytes 196616 | tf_op jit(solution)/shard_map/ppermute | solution.py:434
  53.4 0.6 copy-start.3
  53.4 0.7 copy-start
  54.1 0.7 copy-start.1
  56.6 20.1 %copy-start.6 = (f32[84,8,128]{2,1,0:T(8,128)S(1)}, f32[84,8,128]{2,1,0:T(8,128)}, u32[]{:S(2)}) copy-start(f32[84,8,128]{2,1,0:T(8,128)} %get-tuple-element.12) | copy-start | bytes 1032196
  56.6 40.6 %collective-permute-start.6 = (f32[88,8,128]{2,1,0:T(8,128)}, f32[88,8,128]{2,1,0:T(8,128)S(1)}, u32[]{:S(2)}, u32[]{:S(2)}) collective-permute-start(f32[88,8,128]{2,1,0:T(8,128)} %shard_map.96.own.halo), channel_id=1, source_target_pairs={{4,0},{8,4},{12,8},{16,12},{20,16},{24,20},{28,24},{32,28},{36,32}... | collective-permute-start | bytes 1081352 | tf_op jit(solution)/shard_map/ppermute | solution.py:415
  60.2 38.9 %collective-permute-start.5 = (f32[88,8,128]{2,1,0:T(8,128)}, f32[88,8,128]{2,1,0:T(8,128)S(1)}, u32[]{:S(2)}, u32[]{:S(2)}) collective-permute-start(f32[88,8,128]{2,1,0:T(8,128)} %shard_map.96.own.halo), channel_id=1, source_target_pairs={{0,4},{4,8},{8,12},{12,16},{16,20},{20,24},{24,28},{28,32},{32,36}... | collective-permute-start | bytes 1081352 | tf_op jit(solution)/shard_map/ppermute | solution.py:415
  68.6 28.6 %copy-start.9 = (f32[6,3,16,128]{3,2,1,0:T(8,128)S(1)}, f32[6,3,16,128]{3,2,1,0:T(8,128)}, u32[]{:S(2)}) copy-start(f32[6,3,16,128]{3,2,1,0:T(8,128)} %get-tuple-element.18) | copy-start | bytes 442372
  68.6 14.2 %collective-permute-start.9 = (f32[2,3,16,128]{3,2,1,0:T(8,128)}, f32[2,3,16,128]{3,2,1,0:T(8,128)S(1)}, u32[]{:S(2)}, u32[]{:S(2)}) collective-permute-start(f32[2,3,16,128]{3,2,1,0:T(8,128)} %get-tuple-element.19), channel_id=1, source_target_pairs={{0,8},{4,12},{8,16},{12,20},{16,24},{20,28},{24,32},{28,36},{32,40... | collective-permute-start | bytes 147464 | tf_op jit(solution)/shard_map/ppermute | solution.py:415
  76.7 22.4 %copy-start.14 = (f32[2,3,16,128]{3,2,1,0:T(8,128)S(1)}, f32[2,3,16,128]{3,2,1,0:T(8,128)}, u32[]{:S(2)}) copy-start(f32[2,3,16,128]{3,2,1,0:T(8,128)} %get-tuple-element.20) | copy-start | bytes 147460
  76.7 42.0 %collective-permute-start.1 = (f32[84,8,128]{2,1,0:T(8,128)S(1)}, f32[84,8,128]{2,1,0:T(8,128)S(1)}, u32[]{:S(2)}, u32[]{:S(2)}) collective-permute-start(f32[84,8,128]{2,1,0:T(8,128)S(1)} %copy-done.6), channel_id=1, source_target_pairs={{4,0},{8,4},{12,8},{16,12},{20,16},{24,20},{28,24},{32,28},{36,32}... | collective-permute-start | bytes 1032200 | tf_op jit(solution)/shard_map/ppermute | solution.py:415
  78.8 40.0 %collective-permute-start = (f32[84,8,128]{2,1,0:T(8,128)S(1)}, f32[84,8,128]{2,1,0:T(8,128)S(1)}, u32[]{:S(2)}, u32[]{:S(2)}) collective-permute-start(f32[84,8,128]{2,1,0:T(8,128)S(1)} %copy-done.6), channel_id=1, source_target_pairs={{0,4},{4,8},{8,12},{12,16},{16,20},{20,24},{24,28},{28,32},{32,36}... | collective-permute-start | bytes 1032200 | tf_op jit(solution)/shard_map/ppermute | solution.py:415
  82.8 18.3 %copy-start.2 = (f32[64,512]{1,0:T(8,128)}, f32[64,512]{1,0:T(8,128)S(1)}, u32[]{:S(2)}) copy-start(f32[64,512]{1,0:T(8,128)S(1)} %concatenate.18.first) | copy-start | bytes 393220
  82.8 21.4 %copy-start.13 = (f32[2,3,16,128]{3,2,1,0:T(8,128)}, f32[2,3,16,128]{3,2,1,0:T(8,128)S(1)}, u32[]{:S(2)}) copy-start(f32[2,3,16,128]{3,2,1,0:T(8,128)S(1)} %collective-permute-done.9.force_m2) | copy-start | bytes 147460
  82.8 6.9 %collective-permute-start.16 = (f32[64,512]{1,0:T(8,128)S(1)}, f32[64,512]{1,0:T(8,128)S(1)}, u32[]{:S(2)}, u32[]{:S(2)}) collective-permute-start(f32[64,512]{1,0:T(8,128)S(1)} %concatenate.18.first), channel_id=1, source_target_pairs={{0,32},{4,36},{8,40},{12,44},{16,48},{20,52},{24,56},{28,60},{32,0... | collective-permute-start | bytes 393224 | tf_op jit(solution)/shard_map/ppermute | solution.py:434
  89.7 11.4 %copy-start.12 = (f32[64,512]{1,0:T(8,128)}, f32[64,512]{1,0:T(8,128)S(1)}, u32[]{:S(2)}) copy-start(f32[64,512]{1,0:T(8,128)S(1)} %collective-permute-done.16.second) | copy-start | bytes 393220
  89.7 22.7 %collective-permute-start.7 = (f32[6,3,16,128]{3,2,1,0:T(8,128)}, f32[6,3,16,128]{3,2,1,0:T(8,128)S(1)}, u32[]{:S(2)}, u32[]{:S(2)}) collective-permute-start(f32[6,3,16,128]{3,2,1,0:T(8,128)} %get-tuple-element.17), channel_id=1, source_target_pairs={{0,4},{4,8},{8,12},{12,16},{16,20},{20,24},{24,28},{28,32},{32,36}... | collective-permute-start | bytes 442376 | tf_op jit(solution)/shard_map/ppermute | solution.py:415
  97.1 3.9 %copy-start.4 = (f32[88,8,128]{2,1,0:T(8,128)}, f32[88,8,128]{2,1,0:T(8,128)S(1)}, u32[]{:S(2)}) copy-start(f32[88,8,128]{2,1,0:T(8,128)S(1)} %collective-permute-done.6.down.halo_down) | copy-start | bytes 1081348
  97.2 19.4 %collective-permute-start.8 = (f32[6,3,16,128]{3,2,1,0:T(8,128)S(1)}, f32[6,3,16,128]{3,2,1,0:T(8,128)S(1)}, u32[]{:S(2)}, u32[]{:S(2)}) collective-permute-start(f32[6,3,16,128]{3,2,1,0:T(8,128)S(1)} %copy-done.9), channel_id=1, source_target_pairs={{4,0},{8,4},{12,8},{16,12},{20,16},{24,20},{28,24},{32,28},{36,32}... | collective-permute-start | bytes 442376 | tf_op jit(solution)/shard_map/ppermute | solution.py:415
  99.1 2.0 %copy-start.5 = (f32[88,8,128]{2,1,0:T(8,128)}, f32[88,8,128]{2,1,0:T(8,128)S(1)}, u32[]{:S(2)}) copy-start(f32[88,8,128]{2,1,0:T(8,128)S(1)} %collective-permute-done.5.up.halo_up) | copy-start | bytes 1081348
  99.1 11.1 %collective-permute-start.10 = (f32[2,3,16,128]{3,2,1,0:T(8,128)S(1)}, f32[2,3,16,128]{3,2,1,0:T(8,128)S(1)}, u32[]{:S(2)}, u32[]{:S(2)}) collective-permute-start(f32[2,3,16,128]{3,2,1,0:T(8,128)S(1)} %copy-done.14), channel_id=1, source_target_pairs={{8,0},{12,4},{16,8},{20,12},{24,16},{28,20},{32,24},{36,28},{40,32... | collective-permute-start | bytes 147464 | tf_op jit(solution)/shard_map/ppermute | solution.py:415
  110.2 15.9 %copy-start.15 = (f32[2,3,16,128]{3,2,1,0:T(8,128)}, f32[2,3,16,128]{3,2,1,0:T(8,128)S(1)}, u32[]{:S(2)}) copy-start(f32[2,3,16,128]{3,2,1,0:T(8,128)S(1)} %collective-permute-done.10.force_p2) | copy-start | bytes 147460
  110.2 8.6 %collective-permute-start.19 = (f32[48,128]{1,0:T(8,128)}, f32[48,128]{1,0:T(8,128)S(1)}, u32[]{:S(2)}, u32[]{:S(2)}) collective-permute-start(f32[48,128]{1,0:T(8,128)} %shard_map.100.v0), channel_id=1, source_target_pairs={{0,3},{1,0},{2,1},{3,2},{4,7},{5,4},{6,5},{7,6},{8,11},{9,8},{10,9... | collective-permute-start | bytes 73736 | tf_op jit(solution)/shard_map/ppermute | solution.py:419
  112.3 13.8 %copy-start.10 = (f32[6,3,16,128]{3,2,1,0:T(8,128)}, f32[6,3,16,128]{3,2,1,0:T(8,128)S(1)}, u32[]{:S(2)}) copy-start(f32[6,3,16,128]{3,2,1,0:T(8,128)S(1)} %collective-permute-done.7.force_m1) | copy-start | bytes 442372
  112.3 9.8 %collective-permute-start.18 = (f32[48,128]{1,0:T(8,128)}, f32[48,128]{1,0:T(8,128)S(1)}, u32[]{:S(2)}, u32[]{:S(2)}) collective-permute-start(f32[48,128]{1,0:T(8,128)} %shard_map.100.v0), channel_id=1, source_target_pairs={{0,2},{1,3},{2,0},{3,1},{4,6},{5,7},{6,4},{7,5},{8,10},{9,11},{10,... | collective-permute-start | bytes 73736 | tf_op jit(solution)/shard_map/ppermute | solution.py:419
  116.6 9.5 %copy-start.11 = (f32[6,3,16,128]{3,2,1,0:T(8,128)}, f32[6,3,16,128]{3,2,1,0:T(8,128)S(1)}, u32[]{:S(2)}) copy-start(f32[6,3,16,128]{3,2,1,0:T(8,128)S(1)} %collective-permute-done.8.force_p1) | copy-start | bytes 442372
  116.6 9.5 %collective-permute-start.17 = (f32[48,128]{1,0:T(8,128)}, f32[48,128]{1,0:T(8,128)S(1)}, u32[]{:S(2)}, u32[]{:S(2)}) collective-permute-start(f32[48,128]{1,0:T(8,128)} %shard_map.100.v0), channel_id=1, source_target_pairs={{0,1},{1,2},{2,3},{3,0},{4,5},{5,6},{6,7},{7,4},{8,9},{9,10},{10,1... | collective-permute-start | bytes 73736 | tf_op jit(solution)/shard_map/ppermute | solution.py:419
  118.8 7.4 %copy-start.7 = (f32[84,8,128]{2,1,0:T(8,128)}, f32[84,8,128]{2,1,0:T(8,128)S(1)}, u32[]{:S(2)}) copy-start(f32[84,8,128]{2,1,0:T(8,128)S(1)} %collective-permute-done.1.down) | copy-start | bytes 1032196
  118.8 7.4 %copy-start.8 = (f32[84,8,128]{2,1,0:T(8,128)}, f32[84,8,128]{2,1,0:T(8,128)S(1)}, u32[]{:S(2)}) copy-start(f32[84,8,128]{2,1,0:T(8,128)S(1)} %collective-permute-done.up) | copy-start | bytes 1032196
  118.8 7.4 %copy-start.16 = (f32[48,128]{1,0:T(8,128)}, f32[48,128]{1,0:T(8,128)S(1)}, u32[]{:S(2)}) copy-start(f32[48,128]{1,0:T(8,128)S(1)} %collective-permute-done.19.v3) | copy-start | bytes 73732
  122.2 4.0 %copy-start.17 = (f32[48,128]{1,0:T(8,128)}, f32[48,128]{1,0:T(8,128)S(1)}, u32[]{:S(2)}) copy-start(f32[48,128]{1,0:T(8,128)S(1)} %collective-permute-done.18.v2) | copy-start | bytes 73732
  126.1 0.6 copy-start.18
where the time goes:
time: 137 us; the launch traced here: 136 us
  starting transfers between devices  82.9 us (61%)
  Pallas kernels  31.3 us (23%)
  waiting for transfers between devices  18.4 us (13%)
  local copies, waits for them, and re-layouts  1.97 us (1%)
    ppermute x6, starting transfers between devices, cross_shift(): lax.ppermute(value, 'cross', [(s, (s + steps) % CROSS) for s in range(CRO...  35.4 us
    ppermute x8, starting transfers between devices, slab_shift(): return lax.ppermute(value, 'slab', pairs)  31.4 us
    ppermute x5, starting transfers between devices, exchange_masked(): lax.ppermute(value, 'slab', [(s, s ^ mask) for s in range(lax.axis_size('...  14.8 us
    pallas_call x1, Pallas kernels, on_device(): call(steps_kernel, (struct(*populations.shape), struct(3, *populations.sh...  8.87 us
    ppermute x6, waiting for transfers between devices, cross_shift(): lax.ppermute(value, 'cross', [(s, (s + steps) % CROSS) for s in range(CRO...  7.34 us
    ppermute x8, waiting for transfers between devices, slab_shift(): return lax.ppermute(value, 'slab', pairs)  6.1 us
    pallas_call x1, Pallas kernels, on_device(): call(spread_last_kernel, tuple((struct(n, 3, WIDE, ROWS) for n in counts)...  6 us
    pallas_call x1, Pallas kernels, on_device(): call(spread_first_kernel, struct(768, ROWS), grid=(1,), in_specs=[half_sp...  5.81 us
  transfers between devices with their start and end apart: 20, of which 4 were waited for; matrix products, arithmetic and copies ran while one was open for 0% of the time, Pallas kernels for 15%

commit v1 on v0

--- a/solution.py
+++ b/solution.py
@@ -39,19 +39,16 @@
 DEEP = PLANES + 2 * STEPS
 WIDE = COLUMNS + 2 * STEPS
 CROSS = 4
-GROUP = 32
-MASKS = (4, 16, 2, 1, 8)
 NODES = 768
 MEMBRANES = 16
-VMEM_LIMIT = 56 * 1024 * 1024
-
-
-def call(body, outs, scratch=(), flops=0, **more):
+
+
+def call(body, outs, scratch=(), flops=0, limit=16, **more):
     return pl.pallas_call(
         body,
         out_shape=outs,
         scratch_shapes=list(scratch),
-        compiler_params=pltpu.CompilerParams(vmem_limit_bytes=VMEM_LIMIT),
+        compiler_params=pltpu.CompilerParams(vmem_limit_bytes=limit << 20),
         cost_estimate=pl.CostEstimate(flops=flops, bytes_accessed=1 << 20, transcendentals=0),
         **more,
     )
@@ -61,9 +58,8 @@
     return jax.ShapeDtypeStruct(shape, dtype)
 
 
-def pack_kernel(pops, relax, mask, iface, coarse, own_o, right_o, left_o, iface_o, coarse_o):
+def pack_kernel(pops, relax, mask, iface, right_o, left_o):
     def put(field, z, value):
-        own_o[field * 4 + z] = value
         low = (z % 2) * 4
         right_o[field * 2 + z // 2, low : low + 4] = value[4:8]
         left_o[field * 2 + z // 2, low : low + 4] = value[0:4]
@@ -73,33 +69,31 @@
             put(q, z, pops[q, z])
         put(19, z, relax[z])
         put(20, z, mask[z].astype(F32))
-    tile = jnp.zeros((8, ROWS), F32)
-    iface_o[...] = tile
-    iface_o[0:3] = iface[...].astype(F32)
-    right_o[42] = iface_o[...]
-    left_o[42] = iface_o[...]
-    for sub in range(4):
-        for mom in range(4):
-            coarse_o[sub : sub + 1, mom * 128 : (mom + 1) * 128] = coarse[
-                mom : mom + 1, sub * 128 : (sub + 1) * 128
-            ]
-
-
-def halo_kernel(from_left, from_right, iface_far, iface_own, halo_o):
-    k = lax.axis_index("cross")
-    has_right = jnp.where(k < CROSS - 1, 1.0, 0.0).astype(F32)
-    has_left = jnp.where(k > 0, 1.0, 0.0).astype(F32)
+    for out in (right_o, left_o):
+        out[42] = jnp.zeros((8, ROWS), F32)
+        out[42, 0:3] = iface[...].astype(F32)
+
+
+def wide_kernel(pops, relax, mask, iface, force, from_left, from_right, wide_o):
+    for p in range(8):
+        wide_o[86 + p * 3 : 89 + p * 3] = force[p]
+    for z in range(PLANES):
+        for q in range(19):
+            wide_o[q * 4 + z, 0:8] = pops[q, z]
+        wide_o[76 + z, 0:8] = relax[z]
+        wide_o[80 + z, 0:8] = mask[z].astype(F32)
     for tile in range(42):
-        right = from_right[tile] * has_right
-        left = from_left[tile] * has_left
-        halo_o[2 * tile, 0:4] = right[0:4]
-        halo_o[2 * tile + 1, 0:4] = right[4:8]
-        halo_o[2 * tile, 4:8] = left[0:4]
-        halo_o[2 * tile + 1, 4:8] = left[4:8]
-    halo_o[84 + k] = iface_own[...]
-    halo_o[84 + (k + 1) % 4] = from_right[42]
-    halo_o[84 + (k + 3) % 4] = from_left[42]
-    halo_o[84 + (k + 2) % 4] = iface_far[...]
+        right = from_right[tile]
+        left = from_left[tile]
+        wide_o[2 * tile, 8:12] = right[0:4]
+        wide_o[2 * tile + 1, 8:12] = right[4:8]
+        wide_o[2 * tile, 12:16] = left[0:4]
+        wide_o[2 * tile + 1, 12:16] = left[4:8]
+    wide_o[84, 0:8] = from_left[42]
+    wide_o[84, 8:16] = jnp.zeros((8, ROWS), F32)
+    wide_o[84, 8:11] = iface[...].astype(F32)
+    wide_o[85, 0:8] = from_right[42]
+    wide_o[85, 8:16] = jnp.zeros((8, ROWS), F32)
 
 
 def nodal_kernel(positions, triangles, tension, out, x_s, table_s):
@@ -173,53 +167,51 @@
     out[...] = spread_body(nodes, jnp.zeros((768, ROWS), F32), None)
 
 
-def spread_last_kernel(nodes, partial, own_o, up_o, down_o, up2_o, down2_o):
+def spread_last_kernel(nodes, partial, own_o, up2_o, down2_o):
     total = spread_body(nodes, partial[...], None)
     for p in range(8):
         for d in range(3):
             low = p * 96 + d * 16
             value = total[low : low + 16] + total[low + 48 : low + 64]
             own_o[p, d] = value
-            if p >= 2:
-                up_o[p - 2, d] = value
-            if p < 6:
-                down_o[p, d] = value
             if p >= 6:
                 up2_o[p - 6, d] = value
             if p < 2:
                 down2_o[p, d] = value
 
 
-def lookup_kernel(first, second, up, own, down, out):
-    k = lax.axis_index("cross")
-    place = lax.rem(lax.axis_index("slab"), GROUP)
-    table = jnp.concatenate([first[...], second[...]], axis=0).T
-    high = table.astype(BF16)
-    low = (table - high.astype(F32)).astype(BF16)
-    lhs = jnp.concatenate([high, low], axis=1)
-    ids = lax.broadcasted_iota(I32, (128, 256), 0)
+def lookup_kernel(table, other, up, own, down, out):
+    core = lax.rem(lax.axis_index("cross"), 2)
+    slabs = table.shape[0] // 8
+    lhs = []
+    for part in range(2):
+        for source in (table, other):
+            for quarter in range(2):
+                pieces = []
+                for mom in range(4):
+                    value = source[pl.ds(mom * 2 + quarter, slabs, stride=8)]
+                    high = value.astype(BF16)
+                    pieces.append(high if part == 0 else (value - high.astype(F32)).astype(BF16))
+                lhs.append(jnp.concatenate(pieces, axis=0))
+    lhs = jnp.concatenate(lhs, axis=1)
+    ids = lax.broadcasted_iota(I32, (512, 256), 0)
+    slab_ids = lax.broadcasted_iota(I32, (slabs, 256), 0)
     for d, source in enumerate((up, own, down)):
-        for a in range(CROSS):
-            tile = source[a].astype(I32)
+        for e in range(3):
+            tile = source[e // 2, (e % 2) * 8 : (e % 2) * 8 + 8].astype(I32)
             cell = jnp.concatenate([tile[1:2], tile[2:3]], axis=1)
-            shard = cell >> 9
-            apart = (shard & (GROUP - 1)) ^ place
-            block = jnp.zeros_like(cell)
-            for bit, mask in enumerate(MASKS):
-                block = block + jnp.where((apart & mask) != 0, 1 << bit, 0)
-            row = block * 4 + ((cell >> 7) & 3)
-            row = jnp.where((shard >> 5) == k, row, -1)
-            lane = cell & 127
-            hot = jnp.where(ids == row, 1.0, 0.0).astype(BF16)
+            hot = jnp.where(ids == ((cell & 511) ^ (core * 256)), 1.0, 0.0).astype(BF16)
             found = jnp.dot(
                 lhs, jnp.concatenate([hot, hot], axis=0), preferred_element_type=F32
             )
-            chosen = ids == lane
+            chosen = slab_ids == (cell >> 9)
             for mom in range(4):
                 value = jnp.sum(
-                    jnp.where(chosen, found[mom * 128 : mom * 128 + 128], 0.0), axis=0, keepdims=True
+                    jnp.where(chosen, found[mom * slabs : (mom + 1) * slabs], 0.0),
+                    axis=0,
+                    keepdims=True,
                 )
-                at = (d * CROSS + a) * 4 + mom
+                at = (d * 3 + e) * 4 + mom
                 out[at : at + 1] = 0.75 * value[:, 0:128] + 0.25 * value[:, 128:256]
 
 
@@ -264,54 +256,44 @@
 
 
 def steps_kernel(
-    pops, relax, mask, up, down, halo, halo_up, halo_down,
-    force, force_m1, force_p1, force_m2, force_p2, v0, v1, v2, v3,
+    own, up, down, force_m2, force_p2, found,
     pops_o, flow_o,
-    f_s, g_s, edge_s, hit_s, relax_s, mask_s, force_s, dense_s,
+    f_s, g_s, edge_s, hit_s, relax_s, mask_s, force_s,
 ):
     j = lax.axis_index("slab")
     k = lax.axis_index("cross")
     slabs = lax.axis_size("slab")
-    for q in range(19):
-        span = slice(q * 4, q * 4 + 4)
-        f_s[q, 5:9, 0:8] = pops[q]
-        f_s[q, 5:9, 8:16] = halo[span]
-        f_s[q, 1:5, 0:8] = up[span]
-        f_s[q, 1:5, 8:16] = halo_up[span]
-        f_s[q, 9:13, 0:8] = down[span]
-        f_s[q, 9:13, 8:16] = halo_down[span]
-    for field, dest in ((19, relax_s), (20, mask_s)):
-        span = slice(field * 4, field * 4 + 4)
-        dest[4:8, 0:8] = relax[...] if field == 19 else mask[...].astype(F32)
-        dest[4:8, 8:16] = halo[span]
-        dest[0:4, 0:8] = up[span]
-        dest[0:4, 8:16] = halo_up[span]
-        dest[8:12, 0:8] = down[span]
-        dest[8:12, 8:16] = halo_down[span]
+    for low, source in ((0, up), (4, own), (8, down)):
+        for q in range(19):
+            f_s[q, low + 1 : low + 5] = source[q * 4 : q * 4 + 4]
+        relax_s[low : low + 4] = source[76:80]
+        mask_s[low : low + 4] = source[80:84]
     for p in range(DEEP):
         inverse = 1.0 / relax_s[p]
         for d in range(3):
             value = None
-            for part, low in ((force, 2), (force_m1, 0), (force_p1, 6), (force_m2, 0), (force_p2, 10)):
-                if low <= p < low + part.shape[0]:
-                    value = part[p - low, d] if value is None else value + part[p - low, d]
+            for part, shift in ((own, -2), (up, 2), (down, -6)):
+                if 0 <= p + shift < 8:
+                    more = part[86 + (p + shift) * 3 + d]
+                    value = more if value is None else value + more
+            for part, low in ((force_m2, 0), (force_p2, 10)):
+                if low <= p < low + 2:
+                    value = value + part[p - low, d]
             force_s[p, d] = value * inverse
 
-    values = v0[...] + v1[...] + v2[...] + v3[...]
-    dense_s[...] = values
     rows64 = lax.broadcasted_iota(I32, (64, 128), 0)
     rows128 = lax.broadcasted_iota(I32, (128, 128), 0)
     ids = lax.broadcasted_iota(I32, (WIDE, ROWS), 0)
-    for d, source in enumerate((halo_up, halo, halo_down)):
+    for d, source in enumerate((up, own, down)):
         slab_there = (j + d - 1 >= 0) & (j + d - 1 < slabs)
         lhs = []
         rhs = []
         for e in (-1, 0, 1):
             member = k + e
             there = slab_there & (member >= 0) & (member < CROSS)
-            member = jnp.clip(member, 0, CROSS - 1)
-            cell = source[84 + member].astype(I32)[0:1]
-            amounts = dense_s[pl.ds(pl.multiple_of((d * CROSS + member) * 4, 4), 4)]
+            at = e + 1
+            cell = source[84 + at // 2, (at % 2) * 8 : (at % 2) * 8 + 1].astype(I32)
+            amounts = found[(d * 3 + at) * 4 : (d * 3 + at) * 4 + 4]
             column = (cell >> 7) & 7
             if e == 0:
                 place = column
@@ -416,45 +398,23 @@
 
 
 def cross_shift(value, steps):
-    return lax.ppermute(value, "cross", [(s, (s + steps) % CROSS) for s in range(CROSS)])
-
-
-def swap_group_and_cross(value):
-    pairs = []
-    for group in range(CROSS):
-        for place in range(GROUP):
-            for k in range(CROSS):
-                pairs.append(
-                    ((group * GROUP + place) * CROSS + k, (k * GROUP + place) * CROSS + group)
-                )
-    return lax.ppermute(value, ("slab", "cross"), pairs)
-
-
-def exchange_masked(value, mask):
-    return lax.ppermute(value, "slab", [(s, s ^ mask) for s in range(lax.axis_size("slab"))])
+    pairs = [(s, s + steps) for s in range(CROSS) if 0 <= s + steps < CROSS]
+    return lax.ppermute(value, "cross", pairs)
 
 
 def on_device(
     populations, fluid_mask, relaxation, positions, triangles, tension, coarse_moments, interface
 ):
-    own, to_right, to_left, iface, shard = call(
-        pack_kernel,
-        (struct(84, 8, ROWS), struct(43, 8, ROWS), struct(43, 8, ROWS), struct(8, ROWS), struct(4, 512)),
-    )(populations, relaxation, fluid_mask, interface, coarse_moments)
-    table = swap_group_and_cross(shard)
+    slabs = lax.axis_size("slab")
+    core = lax.rem(lax.axis_index("cross"), 2)
+    shard = lax.dynamic_index_in_dim(coarse_moments.reshape(4, 2, 2, ROWS), core, 1, keepdims=False)
+    shard = shard.reshape(8, ROWS)
+    table = lax.all_to_all(jnp.broadcast_to(shard[None], (slabs, 8, ROWS)), "slab", 0, 0)
+
+    fields = (populations, relaxation, fluid_mask, interface)
+    to_right, to_left = call(pack_kernel, (struct(43, 8, ROWS), struct(43, 8, ROWS)))(*fields)
     from_left = cross_shift(to_right, 1)
     from_right = cross_shift(to_left, -1)
-    iface_far = cross_shift(iface, 2)
-    up = slab_shift(own, 1)
-    down = slab_shift(own, -1)
-    for mask in MASKS[:-1]:
-        table = jnp.concatenate([table, exchange_masked(table, mask)], axis=0)
-    other = exchange_masked(table, MASKS[-1])
-
-    halo = call(halo_kernel, struct(88, 8, ROWS))(from_left, from_right, iface_far, iface)
-    halo_up = slab_shift(halo, 1)
-    halo_down = slab_shift(halo, -1)
-
     nodes = call(
         nodal_kernel,
         struct(MEMBRANES, 8, NODES),
@@ -478,8 +438,8 @@
         out_specs=whole_spec(768, ROWS),
         flops=1 << 31,
     )(nodes)
-    counts = (8, 6, 6, 2, 2)
-    force, to_up, to_down, to_up2, to_down2 = call(
+    counts = (8, 2, 2)
+    force, to_up2, to_down2 = call(
         spread_last_kernel,
         tuple(struct(n, 3, WIDE, ROWS) for n in counts),
         grid=(1,),
@@ -487,23 +447,22 @@
         out_specs=tuple(whole_spec(n, 3, WIDE, ROWS) for n in counts),
         flops=1 << 31,
     )(nodes, partial)
-    force_m1 = slab_shift(to_up, 1)
-    force_p1 = slab_shift(to_down, -1)
+    wide = call(wide_kernel, struct(110, WIDE, ROWS))(*fields, force, from_left, from_right)
+    wide_up = slab_shift(wide, 1)
+    wide_down = slab_shift(wide, -1)
     force_m2 = slab_shift(to_up2, 2)
     force_p2 = slab_shift(to_down2, -2)
-
-    tail = pl.BlockSpec((4, 8, ROWS), lambda i: (21, 0, 0))
+    other = lax.ppermute(table, "cross", [(s, s ^ 1) for s in range(CROSS)])
+
+    tail = pl.BlockSpec((2, WIDE, ROWS), lambda i: (42, 0, 0))
     found = call(
         lookup_kernel,
-        struct(48, ROWS),
+        struct(36, ROWS),
         grid=(1,),
-        in_specs=[whole_spec(64, 512), whole_spec(64, 512), tail, tail, tail],
-        out_specs=whole_spec(48, ROWS),
+        in_specs=[whole_spec(slabs * 8, ROWS), whole_spec(slabs * 8, ROWS), tail, tail, tail],
+        out_specs=whole_spec(36, ROWS),
         flops=1 << 30,
-    )(table, other, halo_up, halo, halo_down)
-    found1 = cross_shift(found, 1)
-    found2 = cross_shift(found, 2)
-    found3 = cross_shift(found, 3)
+    )(table.reshape(slabs * 8, ROWS), other.reshape(slabs * 8, ROWS), wide_up, wide, wide_down)
 
     state = pltpu.VMEM((19, DEEP + 2, WIDE, ROWS), F32)
     field = pltpu.VMEM((DEEP, WIDE, ROWS), F32)
@@ -518,12 +477,10 @@
             field,
             field,
             pltpu.VMEM((DEEP, 3, WIDE, ROWS), F32),
-            pltpu.VMEM((48, ROWS), F32),
         ],
         flops=1 << 31,
     )(
-        populations, relaxation, fluid_mask, up, down, halo, halo_up, halo_down,
-        force, force_m1, force_p1, force_m2, force_p2, found, found1, found2, found3,
+        wide, wide_up, wide_down, force_m2, force_p2, found
     )
 
 

time: 137 us -> 80.3 us (0.59)
  the two profiles are of different devices: /device:TPU:54 before, /device:TPU:65 now
where the time goes in v1:
time: 80.3 us; the launch traced here: 79.9 us
  starting transfers between devices  47.4 us (59%)
  Pallas kernels  20.7 us (26%)
  waiting for transfers between devices  9.07 us (11%)
  local copies, waits for them, and re-layouts  1.72 us (2%)
  between operations  0.9 us (1%)
    ppermute x4, starting transfers between devices, slab_shift(): return lax.ppermute(value, 'slab', pairs)  18.7 us
    all_to_all x1, starting transfers between devices, on_device(): lax.all_to_all(jnp.broadcast_to(shard[None], (slabs, 8, ROWS)), 'slab', 0...  15.7 us
    ppermute x2, starting transfers between devices, cross_shift(): return lax.ppermute(value, 'cross', pairs)  11.1 us
    ppermute x4, waiting for transfers between devices, slab_shift(): return lax.ppermute(value, 'slab', pairs)  8.72 us
    pallas_call x1, Pallas kernels, on_device(): call(steps_kernel, (struct(*populations.shape), struct(3, *populations.sh...  7.17 us
    pallas_call x1, Pallas kernels, on_device(): call(spread_last_kernel, tuple((struct(n, 3, WIDE, ROWS) for n in counts)...  4.11 us
    pallas_call x1, Pallas kernels, on_device(): call(spread_first_kernel, struct(768, ROWS), grid=(1,), in_specs=[half_sp...  4.09 us
    pallas_call x1, Pallas kernels, on_device(): call(lookup_kernel, struct(36, ROWS), grid=(1,), in_specs=[whole_spec(sla...  3.12 us
  transfers between devices with their start and end apart: 8, of which 2 were waited for; matrix products, arithmetic and copies ran while one was open for 0% of the time, Pallas kernels for 17%

profile of v1, /device:TPU:65, one launch (start us, length us, event | category | flops | bytes accessed | tf_op | source)
XLA Modules:
  0.0 79.9 jit_solution(7984820650135069222)
XLA Ops:
  0.6 0.0 copy-start.9
  0.6 0.7 copy-done.9
  1.4 0.8 %broadcast_in_dim.8 = f32[128,8,128]{2,1,0:T(8,128)} broadcast(f32[8,128]{1,0:T(8,128)S(1)} %bitcast.5), dimensions={1,2} | broadcast | bytes 528384 | tf_op jit(solution)/shard_map/broadcast_in_dim | solution.py:412
  2.2 0.0 copy-start
  2.2 0.0 copy-start.1
  2.2 0.0 copy-start.2
  2.2 0.0 copy-start.3
  2.2 15.7 %all-to-all-start = ((f32[128,8,128]{2,1,0:T(8,128)}), f32[128,8,128]{2,1,0:T(8,128)S(1)}, u32[]{:S(2)}, u32[]{:S(2)}) async-start(f32[128,8,128]{2,1,0:T(8,128)} %broadcast_in_dim.8), calls=%async_computation | async-start | bytes 1048576 | tf_op jit(solution)/shard_map/all_to_all | solution.py:412
  17.9 0.0 copy-done
  17.9 0.0 copy-done.1
  17.9 0.0 copy-done.2
  17.9 0.0 copy-done.3
  17.9 0.0 copy-start.4
  17.9 0.0 copy-start.5
  17.9 0.0 copy-start.8
  18.0 9.2 %collective-permute-start = (f32[43,8,128]{2,1,0:T(8,128)S(1)}, f32[43,8,128]{2,1,0:T(8,128)S(1)}, u32[]{:S(2)}, u32[]{:S(2)}) collective-permute-start(f32[43,8,128]{2,1,0:T(8,128)S(1)} %get-tuple-element.8), channel_id=1, source_target_pairs={{0,1},{1,2},{2,3},{4,5},{5,6},{6,7},{8,9},{9,10},{10,11},{12,13},{... | collective-permute-start | bytes 528392 | tf_op jit(solution)/shard_map/ppermute | solution.py:402
  27.2 1.9 %collective-permute-start.1 = (f32[43,8,128]{2,1,0:T(8,128)S(1)}, f32[43,8,128]{2,1,0:T(8,128)S(1)}, u32[]{:S(2)}, u32[]{:S(2)}) collective-permute-start(f32[43,8,128]{2,1,0:T(8,128)S(1)} %get-tuple-element.9), channel_id=1, source_target_pairs={{1,0},{2,1},{3,2},{5,4},{6,5},{7,6},{9,8},{10,9},{11,10},{13,12},{... | collective-permute-start | bytes 528392 | tf_op jit(solution)/shard_map/ppermute | solution.py:402
  29.1 0.0 copy-done.4
  29.1 0.0 copy-done.5
  29.2 0.0 copy-done.8
  29.2 2.1 %shard_map.95.nodes = f32[16,8,768]{2,1,0:T(8,128)S(1)} custom-call(s32[3,16,642]{2,1,0:T(8,128)S(1)} %copy-done.4, s32[3,1280]{1,0:T(4,128)S(1)} %copy-done.8, f32[16,1280]{1,0:T(8,128)S(1)} %copy-done.5), custom_call_target="tpu_custom_call" | custom-call | flops 1073741824 | bytes 1048576 | tf_op jit(solution)/shard_map/pallas_call | solution.py:418
  31.3 4.1 %shard_map.96.partial = f32[768,128]{1,0:T(8,128)S(1)} custom-call(f32[16,8,768]{2,1,0:T(8,128)S(1)} %shard_map.95.nodes), custom_call_target="tpu_custom_call" | custom-call | flops 2147483648 | bytes 1048576 | tf_op jit(solution)/shard_map/pallas_call | solution.py:433
  35.4 4.1 %shard_map.97 = (f32[8,3,16,128]{3,2,1,0:T(8,128)S(1)}, f32[2,3,16,128]{3,2,1,0:T(8,128)S(1)}, f32[2,3,16,128]{3,2,1,0:T(8,128)S(1)}) custom-call(f32[16,8,768]{2,1,0:T(8,128)S(1)} %shard_map.95.nodes, f32[768,128]{1,0:T(8,128)S(1)} %shard_map.96.partial), custom_call_target="tpu_custom_call" | custom-call | flops 2147483648 | bytes 1048576 | tf_op jit(solution)/shard_map/pallas_call | solution.py:442
  39.5 0.0 copy-start.6
  39.5 0.0 copy-start.7
  39.5 0.0 collective-permute-done.from_left
  39.5 0.3 collective-permute-done.1.from_right
  39.9 0.1 shard_map.99.own
  40.0 0.1 copy-done.6
  40.1 0.0 copy-done.7
  40.1 6.4 %collective-permute-start.3 = (f32[110,16,128]{2,1,0:T(8,128)S(1)}, f32[110,16,128]{2,1,0:T(8,128)S(1)}, u32[]{:S(2)}, u32[]{:S(2)}) collective-permute-start(f32[110,16,128]{2,1,0:T(8,128)S(1)} %shard_map.99.own), channel_id=1, source_target_pairs={{4,0},{8,4},{12,8},{16,12},{20,16},{24,20},{28,24},{32,28},{36,32}... | collective-permute-start | bytes 2703368 | tf_op jit(solution)/shard_map/ppermute | solution.py:397
  46.5 1.9 %collective-permute-start.2 = (f32[110,16,128]{2,1,0:T(8,128)S(1)}, f32[110,16,128]{2,1,0:T(8,128)S(1)}, u32[]{:S(2)}, u32[]{:S(2)}) collective-permute-start(f32[110,16,128]{2,1,0:T(8,128)S(1)} %shard_map.99.own), channel_id=1, source_target_pairs={{0,4},{4,8},{8,12},{12,16},{16,20},{20,24},{24,28},{28,32},{32,36}... | collective-permute-start | bytes 2703368 | tf_op jit(solution)/shard_map/ppermute | solution.py:397
  48.5 0.0 all-to-all-done
  48.5 1.9 %collective-permute-start.6 = (f32[128,8,128]{2,1,0:T(8,128)S(1)}, f32[128,8,128]{2,1,0:T(8,128)S(1)}, u32[]{:S(2)}, u32[]{:S(2)}) collective-permute-start(f32[128,8,128]{2,1,0:T(8,128)S(1)} %all-to-all-done), channel_id=1, source_target_pairs={{0,1},{1,0},{2,3},{3,2},{4,5},{5,4},{6,7},{7,6},{8,9},{9,8},{10,11... | collective-permute-start | bytes 1572872 | tf_op jit(solution)/shard_map/ppermute | solution.py:455
  50.4 1.9 %collective-permute-start.4 = (f32[2,3,16,128]{3,2,1,0:T(8,128)}, f32[2,3,16,128]{3,2,1,0:T(8,128)S(1)}, u32[]{:S(2)}, u32[]{:S(2)}) collective-permute-start(f32[2,3,16,128]{3,2,1,0:T(8,128)} %copy-done.7), channel_id=1, source_target_pairs={{0,8},{4,12},{8,16},{12,20},{16,24},{20,28},{24,32},{28,36},{32,40... | collective-permute-start | bytes 147464 | tf_op jit(solution)/shard_map/ppermute | solution.py:397
  52.3 8.5 %collective-permute-start.5 = (f32[2,3,16,128]{3,2,1,0:T(8,128)}, f32[2,3,16,128]{3,2,1,0:T(8,128)S(1)}, u32[]{:S(2)}, u32[]{:S(2)}) collective-permute-start(f32[2,3,16,128]{3,2,1,0:T(8,128)} %copy-done.6), channel_id=1, source_target_pairs={{8,0},{12,4},{16,8},{20,12},{24,16},{28,20},{32,24},{36,28},{40,32... | collective-permute-start | bytes 147464 | tf_op jit(solution)/shard_map/ppermute | solution.py:397
  60.8 0.0 collective-permute-done.3.down
  60.8 8.7 %collective-permute-done.2.up = f32[110,16,128]{2,1,0:T(8,128)S(1)} collective-permute-done((f32[110,16,128]{2,1,0:T(8,128)S(1)}, f32[110,16,128]{2,1,0:T(8,128)S(1)}, u32[]{:S(2)}, u32[]{:S(2)}) %collective-permute-start.2) | collective-permute-done | bytes 901152 | tf_op jit(solution)/shard_map/ppermute | solution.py:397
  69.5 0.0 collective-permute-done.6
  69.5 3.1 %shard_map.100.found = f32[36,128]{1,0:T(8,128)S(1)} custom-call(f32[1024,128]{1,0:T(8,128)S(1)} %bitcast.3, f32[1024,128]{1,0:T(8,128)S(1)} %bitcast.4, f32[110,16,128]{2,1,0:T(8,128)S(1)} %collective-permute-done.2.up, f32[110,16,128]{2,1,0:T(8,128)S(1)} %shard_map.99.own, f32[110,16,128]{2,1,0:T(8,128)S(1)} %collective-permute-done.3.down), custom_call_target="tpu_custom_call" | custom-call | flops 1073741824 | bytes 1048576 | tf_op jit(solution)/shard_map/pallas_call | solution.py:458
  72.7 0.0 collective-permute-done.4.force_m2
  72.7 0.0 collective-permute-done.5.force_p2
  72.7 7.2 %shard_map.101 = (f32[19,4,8,128]{3,2,1,0:T(8,128)}, f32[3,4,8,128]{3,2,1,0:T(8,128)}) custom-call(f32[110,16,128]{2,1,0:T(8,128)S(1)} %shard_map.99.own, f32[110,16,128]{2,1,0:T(8,128)S(1)} %collective-permute-done.2.up, f32[110,16,128]{2,1,0:T(8,128)S(1)} %collective-permute-done.3.down, f32[2,3,16,128]{3,2,1,0:T(8,128)S(1)} %collective-permute-done.4.force_m2, ...), custom_call_target="tpu_custom_call" | custom-call | flops 2147483648 | bytes 1048576 | tf_op jit(solution)/shard_map/pallas_call | solution.py:469
  (3 shorter events, 0.1 us)
Async XLA Ops:
  0.6 0.7 copy-start.9
  2.2 15.7 %copy-start = (f32[19,4,8,128]{3,2,1,0:T(8,128)S(1)}, f32[19,4,8,128]{3,2,1,0:T(8,128)}, u32[]{:S(2)}) copy-start(f32[19,4,8,128]{3,2,1,0:T(8,128)} %pops.3) | copy-start | bytes 933892
  2.2 15.7 %copy-start.1 = (f32[4,8,128]{2,1,0:T(8,128)S(1)}, f32[4,8,128]{2,1,0:T(8,128)}, u32[]{:S(2)}) copy-start(f32[4,8,128]{2,1,0:T(8,128)} %relax.3) | copy-start | bytes 49156
  2.2 15.7 %copy-start.2 = (s32[4,8,128]{2,1,0:T(8,128)S(1)}, s32[4,8,128]{2,1,0:T(8,128)}, u32[]{:S(2)}) copy-start(s32[4,8,128]{2,1,0:T(8,128)} %mask.3) | copy-start | bytes 49156
  2.2 15.7 %copy-start.3 = (s32[3,128]{1,0:T(4,128)S(1)}, s32[3,128]{1,0:T(4,128)}, u32[]{:S(2)}) copy-start(s32[3,128]{1,0:T(4,128)} %iface.3) | copy-start | bytes 4612
  2.2 46.3 %all-to-all-start = ((f32[128,8,128]{2,1,0:T(8,128)}), f32[128,8,128]{2,1,0:T(8,128)S(1)}, u32[]{:S(2)}, u32[]{:S(2)}) async-start(f32[128,8,128]{2,1,0:T(8,128)} %broadcast_in_dim.8), calls=%async_computation | async-start | bytes 1048576 | tf_op jit(solution)/shard_map/all_to_all | solution.py:412
  17.9 11.2 %copy-start.4 = (s32[3,16,642]{2,1,0:T(8,128)S(1)}, s32[3,16,642]{2,1,0:T(8,128)}, u32[]{:S(2)}) copy-start(s32[3,16,642]{2,1,0:T(8,128)} %positions.1) | copy-start | bytes 369796
  17.9 11.2 %copy-start.5 = (f32[16,1280]{1,0:T(8,128)S(1)}, f32[16,1280]{1,0:T(8,128)}, u32[]{:S(2)}) copy-start(f32[16,1280]{1,0:T(8,128)} %tension.1) | copy-start | bytes 245764
  17.9 11.2 %copy-start.8 = (s32[3,1280]{1,0:T(4,128)S(1)}, s32[3,1280]{1,0:T(4,128)}, u32[]{:S(2)}) copy-start(s32[3,1280]{1,0:T(4,128)} %triangles.1) | copy-start | bytes 46084
  18.0 21.5 %collective-permute-start = (f32[43,8,128]{2,1,0:T(8,128)S(1)}, f32[43,8,128]{2,1,0:T(8,128)S(1)}, u32[]{:S(2)}, u32[]{:S(2)}) collective-permute-start(f32[43,8,128]{2,1,0:T(8,128)S(1)} %get-tuple-element.8), channel_id=1, source_target_pairs={{0,1},{1,2},{2,3},{4,5},{5,6},{6,7},{8,9},{9,10},{10,11},{12,13},{... | collective-permute-start | bytes 528392 | tf_op jit(solution)/shard_map/ppermute | solution.py:402
  27.2 12.7 %collective-permute-start.1 = (f32[43,8,128]{2,1,0:T(8,128)S(1)}, f32[43,8,128]{2,1,0:T(8,128)S(1)}, u32[]{:S(2)}, u32[]{:S(2)}) collective-permute-start(f32[43,8,128]{2,1,0:T(8,128)S(1)} %get-tuple-element.9), channel_id=1, source_target_pairs={{1,0},{2,1},{3,2},{5,4},{6,5},{7,6},{9,8},{10,9},{11,10},{13,12},{... | collective-permute-start | bytes 528392 | tf_op jit(solution)/shard_map/ppermute | solution.py:402
  39.5 0.6 copy-start.6
  39.5 0.6 copy-start.7
  40.1 20.7 %collective-permute-start.3 = (f32[110,16,128]{2,1,0:T(8,128)S(1)}, f32[110,16,128]{2,1,0:T(8,128)S(1)}, u32[]{:S(2)}, u32[]{:S(2)}) collective-permute-start(f32[110,16,128]{2,1,0:T(8,128)S(1)} %shard_map.99.own), channel_id=1, source_target_pairs={{4,0},{8,4},{12,8},{16,12},{20,16},{24,20},{28,24},{32,28},{36,32}... | collective-permute-start | bytes 2703368 | tf_op jit(solution)/shard_map/ppermute | solution.py:397
  46.5 23.0 %collective-permute-start.2 = (f32[110,16,128]{2,1,0:T(8,128)S(1)}, f32[110,16,128]{2,1,0:T(8,128)S(1)}, u32[]{:S(2)}, u32[]{:S(2)}) collective-permute-start(f32[110,16,128]{2,1,0:T(8,128)S(1)} %shard_map.99.own), channel_id=1, source_target_pairs={{0,4},{4,8},{8,12},{12,16},{16,20},{20,24},{24,28},{28,32},{32,36}... | collective-permute-start | bytes 2703368 | tf_op jit(solution)/shard_map/ppermute | solution.py:397
  48.5 21.1 %collective-permute-start.6 = (f32[128,8,128]{2,1,0:T(8,128)S(1)}, f32[128,8,128]{2,1,0:T(8,128)S(1)}, u32[]{:S(2)}, u32[]{:S(2)}) collective-permute-start(f32[128,8,128]{2,1,0:T(8,128)S(1)} %all-to-all-done), channel_id=1, source_target_pairs={{0,1},{1,0},{2,3},{3,2},{4,5},{5,4},{6,7},{7,6},{8,9},{9,8},{10,11... | collective-permute-start | bytes 1572872 | tf_op jit(solution)/shard_map/ppermute | solution.py:455
  50.4 22.3 %collective-permute-start.4 = (f32[2,3,16,128]{3,2,1,0:T(8,128)}, f32[2,3,16,128]{3,2,1,0:T(8,128)S(1)}, u32[]{:S(2)}, u32[]{:S(2)}) collective-permute-start(f32[2,3,16,128]{3,2,1,0:T(8,128)} %copy-done.7), channel_id=1, source_target_pairs={{0,8},{4,12},{8,16},{12,20},{16,24},{20,28},{24,32},{28,36},{32,40... | collective-permute-start | bytes 147464 | tf_op jit(solution)/shard_map/ppermute | solution.py:397
  52.3 20.4 %collective-permute-start.5 = (f32[2,3,16,128]{3,2,1,0:T(8,128)}, f32[2,3,16,128]{3,2,1,0:T(8,128)S(1)}, u32[]{:S(2)}, u32[]{:S(2)}) collective-permute-start(f32[2,3,16,128]{3,2,1,0:T(8,128)} %copy-done.6), channel_id=1, source_target_pairs={{8,0},{12,4},{16,8},{20,12},{24,16},{28,20},{32,24},{36,28},{40,32... | collective-permute-start | bytes 147464 | tf_op jit(solution)/shard_map/ppermute | solution.py:397

commit v2 on v1

--- a/solution.py
+++ b/solution.py
@@ -160,7 +160,7 @@
             lhs, along_row, (((1,), (1,)), ((), ())), preferred_element_type=F32
         )
 
-    return lax.fori_loop(0, nodes.shape[0], add, initial)
+    return lax.fori_loop(0, nodes.shape[0], add, initial, unroll=True)
 
 
 def spread_first_kernel(nodes, out):
@@ -180,8 +180,39 @@
                 down2_o[p, d] = value
 
 
-def lookup_kernel(table, other, up, own, down, out):
+def chunk_kernel(coarse, out):
     core = lax.rem(lax.axis_index("cross"), 2)
+    rows = []
+    for mom in range(4):
+        for quarter in range(2):
+            low = pl.multiple_of(core * 256 + quarter * 128, 128)
+            rows.append(coarse[mom : mom + 1, pl.ds(low, 128)])
+    tile = jnp.concatenate(rows, axis=0)
+    out[...] = jnp.broadcast_to(tile[None], out.shape)
+
+
+def lookup(lhs, source, out, at):
+    core = lax.rem(lax.axis_index("cross"), 2)
+    slabs = lhs.shape[0] // 4
+    ids = lax.broadcasted_iota(I32, (512, 256), 0)
+    slab_ids = lax.broadcasted_iota(I32, (slabs, 256), 0)
+    for e in range(3):
+        tile = source[e // 2, (e % 2) * 8 : (e % 2) * 8 + 8].astype(I32)
+        cell = jnp.concatenate([tile[1:2], tile[2:3]], axis=1)
+        hot = jnp.where(ids == ((cell & 511) ^ (core * 256)), 1.0, 0.0).astype(BF16)
+        found = jnp.dot(lhs, jnp.concatenate([hot, hot], axis=0), preferred_element_type=F32)
+        chosen = slab_ids == (cell >> 9)
+        for mom in range(4):
+            value = jnp.sum(
+                jnp.where(chosen, found[mom * slabs : (mom + 1) * slabs], 0.0),
+                axis=0,
+                keepdims=True,
+            )
+            row = at + e * 4 + mom
+            out[row : row + 1] = 0.75 * value[:, 0:128] + 0.25 * value[:, 128:256]
+
+
+def lookup_own_kernel(table, other, own, out, lhs_o):
     slabs = table.shape[0] // 8
     lhs = []
     for part in range(2):
@@ -194,25 +225,13 @@
                     pieces.append(high if part == 0 else (value - high.astype(F32)).astype(BF16))
                 lhs.append(jnp.concatenate(pieces, axis=0))
     lhs = jnp.concatenate(lhs, axis=1)
-    ids = lax.broadcasted_iota(I32, (512, 256), 0)
-    slab_ids = lax.broadcasted_iota(I32, (slabs, 256), 0)
-    for d, source in enumerate((up, own, down)):
-        for e in range(3):
-            tile = source[e // 2, (e % 2) * 8 : (e % 2) * 8 + 8].astype(I32)
-            cell = jnp.concatenate([tile[1:2], tile[2:3]], axis=1)
-            hot = jnp.where(ids == ((cell & 511) ^ (core * 256)), 1.0, 0.0).astype(BF16)
-            found = jnp.dot(
-                lhs, jnp.concatenate([hot, hot], axis=0), preferred_element_type=F32
-            )
-            chosen = slab_ids == (cell >> 9)
-            for mom in range(4):
-                value = jnp.sum(
-                    jnp.where(chosen, found[mom * slabs : (mom + 1) * slabs], 0.0),
-                    axis=0,
-                    keepdims=True,
-                )
-                at = (d * 3 + e) * 4 + mom
-                out[at : at + 1] = 0.75 * value[:, 0:128] + 0.25 * value[:, 128:256]
+    lhs_o[...] = lhs
+    lookup(lhs, own, out, 0)
+
+
+def lookup_far_kernel(lhs, up, down, out):
+    lookup(lhs[...], up, out, 0)
+    lookup(lhs[...], down, out, 12)
 
 
 def rolled(value, velocity):
@@ -256,7 +275,7 @@
 
 
 def steps_kernel(
-    own, up, down, force_m2, force_p2, found,
+    own, up, down, force_m2, force_p2, found_own, found_far,
     pops_o, flow_o,
     f_s, g_s, edge_s, hit_s, relax_s, mask_s, force_s,
 ):
@@ -284,7 +303,9 @@
     rows64 = lax.broadcasted_iota(I32, (64, 128), 0)
     rows128 = lax.broadcasted_iota(I32, (128, 128), 0)
     ids = lax.broadcasted_iota(I32, (WIDE, ROWS), 0)
+    founds = ((found_far, 0), (found_own, 0), (found_far, 12))
     for d, source in enumerate((up, own, down)):
+        found, found_at = founds[d]
         slab_there = (j + d - 1 >= 0) & (j + d - 1 < slabs)
         lhs = []
         rhs = []
@@ -293,7 +314,7 @@
             there = slab_there & (member >= 0) & (member < CROSS)
             at = e + 1
             cell = source[84 + at // 2, (at % 2) * 8 : (at % 2) * 8 + 1].astype(I32)
-            amounts = found[(d * 3 + at) * 4 : (d * 3 + at) * 4 + 4]
+            amounts = found[found_at + at * 4 : found_at + at * 4 + 4]
             column = (cell >> 7) & 7
             if e == 0:
                 place = column
@@ -376,7 +397,7 @@
                 dest[2 * n + 2, p + 1 - c[0]] = rolled(new_two, tuple(-x for x in c))
             return carry
 
-        lax.fori_loop(step, DEEP - step, plane, 0)
+        lax.fori_loop(step, DEEP - step, plane, 0, unroll=2)
 
     last = f_s if STEPS % 2 == 0 else g_s
     for z in range(PLANES):
@@ -406,10 +427,9 @@
     populations, fluid_mask, relaxation, positions, triangles, tension, coarse_moments, interface
 ):
     slabs = lax.axis_size("slab")
-    core = lax.rem(lax.axis_index("cross"), 2)
-    shard = lax.dynamic_index_in_dim(coarse_moments.reshape(4, 2, 2, ROWS), core, 1, keepdims=False)
-    shard = shard.reshape(8, ROWS)
-    table = lax.all_to_all(jnp.broadcast_to(shard[None], (slabs, 8, ROWS)), "slab", 0, 0)
+    table = lax.all_to_all(
+        call(chunk_kernel, struct(slabs, 8, ROWS))(coarse_moments), "slab", 0, 0
+    )
 
     fields = (populations, relaxation, fluid_mask, interface)
     to_right, to_left = call(pack_kernel, (struct(43, 8, ROWS), struct(43, 8, ROWS)))(*fields)
@@ -455,14 +475,22 @@
     other = lax.ppermute(table, "cross", [(s, s ^ 1) for s in range(CROSS)])
 
     tail = pl.BlockSpec((2, WIDE, ROWS), lambda i: (42, 0, 0))
-    found = call(
-        lookup_kernel,
-        struct(36, ROWS),
+    found_own, lhs = call(
+        lookup_own_kernel,
+        (struct(12, ROWS), struct(4 * slabs, 1024, dtype=BF16)),
         grid=(1,),
-        in_specs=[whole_spec(slabs * 8, ROWS), whole_spec(slabs * 8, ROWS), tail, tail, tail],
-        out_specs=whole_spec(36, ROWS),
+        in_specs=[whole_spec(slabs * 8, ROWS), whole_spec(slabs * 8, ROWS), tail],
+        out_specs=(whole_spec(12, ROWS), whole_spec(4 * slabs, 1024)),
         flops=1 << 30,
-    )(table.reshape(slabs * 8, ROWS), other.reshape(slabs * 8, ROWS), wide_up, wide, wide_down)
+    )(table.reshape(slabs * 8, ROWS), other.reshape(slabs * 8, ROWS), wide)
+    found_far = call(
+        lookup_far_kernel,
+        struct(24, ROWS),
+        grid=(1,),
+        in_specs=[whole_spec(4 * slabs, 1024), tail, tail],
+        out_specs=whole_spec(24, ROWS),
+        flops=1 << 30,
+    )(lhs, wide_up, wide_down)
 
     state = pltpu.VMEM((19, DEEP + 2, WIDE, ROWS), F32)
     field = pltpu.VMEM((DEEP, WIDE, ROWS), F32)
@@ -480,7 +508,7 @@
         ],
         flops=1 << 31,
     )(
-        wide, wide_up, wide_down, force_m2, force_p2, found
+        wide, wide_up, wide_down, force_m2, force_p2, found_own, found_far
     )
 
 

time: 80.3 us -> 75.5 us (0.940)
  Pallas kernels: 20.7 us -> 17.3 us
  local copies, waits for them, and re-layouts: 1.72 us -> 0.74 us
    ppermute x4, waiting for transfers between devices: 8.72 us -> 4.95 us  [slab_shift(): return lax.ppermute(value, 'slab', pairs)]
    ppermute x2, waiting for transfers between devices: 0.35 us -> 3.33 us  [cross_shift(): return lax.ppermute(value, 'cross', pairs)]
    pallas_call x1, Pallas kernels: 4.11 us -> 2.61 us  [on_device(): call(spread_last_kernel, tuple((struct(n, 3, WIDE, ROWS) for n in counts)...]
    pallas_call x1, Pallas kernels: 4.09 us -> 2.61 us  [on_device(): call(spread_first_kernel, struct(768, ROWS), grid=(1,), in_specs=[half_sp...]
    pallas_call x1, Pallas kernels: 7.17 us -> 5.76 us  [on_device(): call(steps_kernel, (struct(*populations.shape), struct(3, *populations.sh...]
    pallas_call x1 -> x3, Pallas kernels: 3.12 us -> 4.08 us  [the longest x1 2.11 us: on_device(): call(lookup_far_kernel, struct(24, ROWS), grid=(1,), in_specs=[whole_spec...]
    broadcast_in_dim x1 -> x0, local copies, waits for them, and re-layouts: 0.83 us -> none  [on_device(): jnp.broadcast_to(shard[None], (slabs, 8, ROWS))]
  transfers between devices with their start and end apart: 8 -> 8, of which waited for: 2 -> 2; matrix products, arithmetic and copies ran while one was open for 0% -> 0% of each run, Pallas kernels for 17% -> 14%
where the time goes in v2:
time: 75.5 us; the launch traced here: 75.1 us
  starting transfers between devices  47.9 us (63%)
  Pallas kernels  17.3 us (23%)
  waiting for transfers between devices  8.29 us (11%)
  between operations  0.91 us (1%)
    ppermute x4, starting transfers between devices, slab_shift(): return lax.ppermute(value, 'slab', pairs)  19.2 us
    all_to_all x1, starting transfers between devices, on_device(): lax.all_to_all(call(chunk_kernel, struct(slabs, 8, ROWS))(coarse_moments)...  15.7 us
    ppermute x2, starting transfers between devices, cross_shift(): return lax.ppermute(value, 'cross', pairs)  11.1 us
    pallas_call x1, Pallas kernels, on_device(): call(steps_kernel, (struct(*populations.shape), struct(3, *populations.sh...  5.76 us
    ppermute x4, waiting for transfers between devices, slab_shift(): return lax.ppermute(value, 'slab', pairs)  4.95 us
    ppermute x2, waiting for transfers between devices, cross_shift(): return lax.ppermute(value, 'cross', pairs)  3.33 us
    pallas_call x1, Pallas kernels, on_device(): call(spread_first_kernel, struct(768, ROWS), grid=(1,), in_specs=[half_sp...  2.61 us
    pallas_call x1, Pallas kernels, on_device(): call(spread_last_kernel, tuple((struct(n, 3, WIDE, ROWS) for n in counts)...  2.61 us
  transfers between devices with their start and end apart: 8, of which 2 were waited for; matrix products, arithmetic and copies ran while one was open for 0% of the time, Pallas kernels for 14%

profile of v2, /device:TPU:65, one launch (start us, length us, event | category | flops | bytes accessed | tf_op | source)
XLA Modules:
  0.0 75.1 jit_solution(18220134919707508482)
XLA Ops:
  0.6 0.0 copy-start.3
  0.6 0.7 copy-done.3
  1.3 0.8 %shard_map.100 = f32[128,8,128]{2,1,0:T(8,128)} custom-call(f32[4,512]{1,0:T(4,128)S(1)} %copy-done.3), custom_call_target="tpu_custom_call" | custom-call | bytes 1048576 | tf_op jit(solution)/shard_map/pallas_call | solution.py:431
  2.2 0.0 copy-start
  2.2 0.0 copy-start.1
  2.2 0.0 copy-start.2
  2.2 0.0 copy-start.4
  2.2 15.7 %all-to-all-start = ((f32[128,8,128]{2,1,0:T(8,128)}), f32[128,8,128]{2,1,0:T(8,128)S(1)}, u32[]{:S(2)}, u32[]{:S(2)}) async-start(f32[128,8,128]{2,1,0:T(8,128)} %shard_map.100), calls=%async_computation | async-start | bytes 1048576 | tf_op jit(solution)/shard_map/all_to_all | solution.py:430
  17.9 0.0 copy-done
  17.9 0.0 copy-done.1
  17.9 0.0 copy-done.2
  17.9 0.0 copy-done.4
  17.9 0.0 copy-start.5
  17.9 0.0 copy-start.6
  17.9 0.0 copy-start.9
  18.0 9.2 %collective-permute-start = (f32[43,8,128]{2,1,0:T(8,128)S(1)}, f32[43,8,128]{2,1,0:T(8,128)S(1)}, u32[]{:S(2)}, u32[]{:S(2)}) collective-permute-start(f32[43,8,128]{2,1,0:T(8,128)S(1)} %get-tuple-element.10), channel_id=1, source_target_pairs={{0,1},{1,2},{2,3},{4,5},{5,6},{6,7},{8,9},{9,10},{10,11},{12,13},{... | collective-permute-start | bytes 528392 | tf_op jit(solution)/shard_map/ppermute | solution.py:423
  27.2 1.9 %collective-permute-start.1 = (f32[43,8,128]{2,1,0:T(8,128)S(1)}, f32[43,8,128]{2,1,0:T(8,128)S(1)}, u32[]{:S(2)}, u32[]{:S(2)}) collective-permute-start(f32[43,8,128]{2,1,0:T(8,128)S(1)} %get-tuple-element.11), channel_id=1, source_target_pairs={{1,0},{2,1},{3,2},{5,4},{6,5},{7,6},{9,8},{10,9},{11,10},{13,12},{... | collective-permute-start | bytes 528392 | tf_op jit(solution)/shard_map/ppermute | solution.py:423
  29.1 0.0 copy-done.5
  29.1 0.0 copy-done.6
  29.1 0.0 copy-done.9
  29.1 2.1 %shard_map.95.nodes = f32[16,8,768]{2,1,0:T(8,128)S(1)} custom-call(s32[3,16,642]{2,1,0:T(8,128)S(1)} %copy-done.5, s32[3,1280]{1,0:T(4,128)S(1)} %copy-done.9, f32[16,1280]{1,0:T(8,128)S(1)} %copy-done.6), custom_call_target="tpu_custom_call" | custom-call | flops 1073741824 | bytes 1048576 | tf_op jit(solution)/shard_map/pallas_call | solution.py:438
  31.2 2.6 %shard_map.96.partial = f32[768,128]{1,0:T(8,128)S(1)} custom-call(f32[16,8,768]{2,1,0:T(8,128)S(1)} %shard_map.95.nodes), custom_call_target="tpu_custom_call" | custom-call | flops 2147483648 | bytes 1048576 | tf_op jit(solution)/shard_map/pallas_call | solution.py:453
  33.9 2.6 %shard_map.97 = (f32[8,3,16,128]{3,2,1,0:T(8,128)S(1)}, f32[2,3,16,128]{3,2,1,0:T(8,128)S(1)}, f32[2,3,16,128]{3,2,1,0:T(8,128)S(1)}) custom-call(f32[16,8,768]{2,1,0:T(8,128)S(1)} %shard_map.95.nodes, f32[768,128]{1,0:T(8,128)S(1)} %shard_map.96.partial), custom_call_target="tpu_custom_call" | custom-call | flops 2147483648 | bytes 1048576 | tf_op jit(solution)/shard_map/pallas_call | solution.py:462
  36.5 0.0 copy-start.7
  36.5 0.0 copy-start.8
  36.5 0.0 collective-permute-done.from_left
  36.5 3.3 %collective-permute-done.1.from_right = f32[43,8,128]{2,1,0:T(8,128)S(1)} collective-permute-done((f32[43,8,128]{2,1,0:T(8,128)S(1)}, f32[43,8,128]{2,1,0:T(8,128)S(1)}, u32[]{:S(2)}, u32[]{:S(2)}) %collective-permute-start.1) | collective-permute-done | bytes 176160 | tf_op jit(solution)/shard_map/ppermute | solution.py:423
  39.8 0.1 shard_map.99.own
  40.0 0.0 copy-done.7
  40.0 0.0 copy-done.8
  40.0 6.7 %collective-permute-start.3 = (f32[110,16,128]{2,1,0:T(8,128)S(1)}, f32[110,16,128]{2,1,0:T(8,128)S(1)}, u32[]{:S(2)}, u32[]{:S(2)}) collective-permute-start(f32[110,16,128]{2,1,0:T(8,128)S(1)} %shard_map.99.own), channel_id=1, source_target_pairs={{4,0},{8,4},{12,8},{16,12},{20,16},{24,20},{28,24},{32,28},{36,32}... | collective-permute-start | bytes 2703368 | tf_op jit(solution)/shard_map/ppermute | solution.py:418
  46.6 1.9 %collective-permute-start.2 = (f32[110,16,128]{2,1,0:T(8,128)S(1)}, f32[110,16,128]{2,1,0:T(8,128)S(1)}, u32[]{:S(2)}, u32[]{:S(2)}) collective-permute-start(f32[110,16,128]{2,1,0:T(8,128)S(1)} %shard_map.99.own), channel_id=1, source_target_pairs={{0,4},{4,8},{8,12},{12,16},{16,20},{20,24},{24,28},{28,32},{32,36}... | collective-permute-start | bytes 2703368 | tf_op jit(solution)/shard_map/ppermute | solution.py:418
  48.6 0.0 all-to-all-done
  48.6 1.9 %collective-permute-start.6 = (f32[128,8,128]{2,1,0:T(8,128)S(1)}, f32[128,8,128]{2,1,0:T(8,128)S(1)}, u32[]{:S(2)}, u32[]{:S(2)}) collective-permute-start(f32[128,8,128]{2,1,0:T(8,128)S(1)} %all-to-all-done), channel_id=1, source_target_pairs={{0,1},{1,0},{2,3},{3,2},{4,5},{5,4},{6,7},{7,6},{8,9},{9,8},{10,11... | collective-permute-start | bytes 1572872 | tf_op jit(solution)/shard_map/ppermute | solution.py:475
  50.5 1.9 %collective-permute-start.4 = (f32[2,3,16,128]{3,2,1,0:T(8,128)}, f32[2,3,16,128]{3,2,1,0:T(8,128)S(1)}, u32[]{:S(2)}, u32[]{:S(2)}) collective-permute-start(f32[2,3,16,128]{3,2,1,0:T(8,128)} %copy-done.8), channel_id=1, source_target_pairs={{0,8},{4,12},{8,16},{12,20},{16,24},{20,28},{24,32},{28,36},{32,40... | collective-permute-start | bytes 147464 | tf_op jit(solution)/shard_map/ppermute | solution.py:418
  52.4 8.7 %collective-permute-start.5 = (f32[2,3,16,128]{3,2,1,0:T(8,128)}, f32[2,3,16,128]{3,2,1,0:T(8,128)S(1)}, u32[]{:S(2)}, u32[]{:S(2)}) collective-permute-start(f32[2,3,16,128]{3,2,1,0:T(8,128)} %copy-done.7), channel_id=1, source_target_pairs={{8,0},{12,4},{16,8},{20,12},{24,16},{28,20},{32,24},{36,28},{40,32... | collective-permute-start | bytes 147464 | tf_op jit(solution)/shard_map/ppermute | solution.py:418
  61.1 0.0 collective-permute-done.6
  61.1 1.1 %shard_map.101 = (f32[12,128]{1,0:T(8,128)S(1)}, bf16[512,1024]{1,0:T(8,128)(2,1)S(1)}) custom-call(f32[1024,128]{1,0:T(8,128)S(1)} %bitcast.2, f32[1024,128]{1,0:T(8,128)S(1)} %bitcast.3, f32[110,16,128]{2,1,0:T(8,128)S(1)} %shard_map.99.own), custom_call_target="tpu_custom_call" | custom-call | flops 1073741824 | bytes 1048576 | tf_op jit(solution)/shard_map/pallas_call | solution.py:478
  62.3 0.0 collective-permute-done.3.down
  62.3 4.9 %collective-permute-done.2.up = f32[110,16,128]{2,1,0:T(8,128)S(1)} collective-permute-done((f32[110,16,128]{2,1,0:T(8,128)S(1)}, f32[110,16,128]{2,1,0:T(8,128)S(1)}, u32[]{:S(2)}, u32[]{:S(2)}) %collective-permute-start.2) | collective-permute-done | bytes 901152 | tf_op jit(solution)/shard_map/ppermute | solution.py:418
  67.2 2.1 %shard_map.102.found_far = f32[24,128]{1,0:T(8,128)S(1)} custom-call(bf16[512,1024]{1,0:T(8,128)(2,1)S(1)} %get-tuple-element.15.lhs, f32[110,16,128]{2,1,0:T(8,128)S(1)} %collective-permute-done.2.up, f32[110,16,128]{2,1,0:T(8,128)S(1)} %collective-permute-done.3.down), custom_call_target="tpu_custom_call" | custom-call | flops 1073741824 | bytes 1048576 | tf_op jit(solution)/shard_map/pallas_call | solution.py:486
  69.3 0.0 collective-permute-done.4.force_m2
  69.3 0.0 collective-permute-done.5.force_p2
  69.3 5.8 %shard_map.103 = (f32[19,4,8,128]{3,2,1,0:T(8,128)}, f32[3,4,8,128]{3,2,1,0:T(8,128)}) custom-call(f32[110,16,128]{2,1,0:T(8,128)S(1)} %shard_map.99.own, f32[110,16,128]{2,1,0:T(8,128)S(1)} %collective-permute-done.2.up, f32[110,16,128]{2,1,0:T(8,128)S(1)} %collective-permute-done.3.down, f32[2,3,16,128]{3,2,1,0:T(8,128)S(1)} %collective-permute-done.4.force_m2, ...), custom_call_target="tpu_custom_call" | custom-call | flops 2147483648 | bytes 1048576 | tf_op jit(solution)/shard_map/pallas_call | solution.py:497
  (1 shorter events, 0.0 us)
Async XLA Ops:
  0.6 0.7 copy-start.3
  2.2 15.7 %copy-start = (f32[19,4,8,128]{3,2,1,0:T(8,128)S(1)}, f32[19,4,8,128]{3,2,1,0:T(8,128)}, u32[]{:S(2)}) copy-start(f32[19,4,8,128]{3,2,1,0:T(8,128)} %pops.3) | copy-start | bytes 933892
  2.2 15.7 %copy-start.1 = (f32[4,8,128]{2,1,0:T(8,128)S(1)}, f32[4,8,128]{2,1,0:T(8,128)}, u32[]{:S(2)}) copy-start(f32[4,8,128]{2,1,0:T(8,128)} %relax.3) | copy-start | bytes 49156
  2.2 15.7 %copy-start.2 = (s32[4,8,128]{2,1,0:T(8,128)S(1)}, s32[4,8,128]{2,1,0:T(8,128)}, u32[]{:S(2)}) copy-start(s32[4,8,128]{2,1,0:T(8,128)} %mask.3) | copy-start | bytes 49156
  2.2 15.7 %copy-start.4 = (s32[3,128]{1,0:T(4,128)S(1)}, s32[3,128]{1,0:T(4,128)}, u32[]{:S(2)}) copy-start(s32[3,128]{1,0:T(4,128)} %iface.3) | copy-start | bytes 4612
  2.2 46.4 %all-to-all-start = ((f32[128,8,128]{2,1,0:T(8,128)}), f32[128,8,128]{2,1,0:T(8,128)S(1)}, u32[]{:S(2)}, u32[]{:S(2)}) async-start(f32[128,8,128]{2,1,0:T(8,128)} %shard_map.100), calls=%async_computation | async-start | bytes 1048576 | tf_op jit(solution)/shard_map/all_to_all | solution.py:430
  17.9 11.2 %copy-start.5 = (s32[3,16,642]{2,1,0:T(8,128)S(1)}, s32[3,16,642]{2,1,0:T(8,128)}, u32[]{:S(2)}) copy-start(s32[3,16,642]{2,1,0:T(8,128)} %positions.1) | copy-start | bytes 369796
  17.9 11.2 %copy-start.6 = (f32[16,1280]{1,0:T(8,128)S(1)}, f32[16,1280]{1,0:T(8,128)}, u32[]{:S(2)}) copy-start(f32[16,1280]{1,0:T(8,128)} %tension.1) | copy-start | bytes 245764
  17.9 11.2 %copy-start.9 = (s32[3,1280]{1,0:T(4,128)S(1)}, s32[3,1280]{1,0:T(4,128)}, u32[]{:S(2)}) copy-start(s32[3,1280]{1,0:T(4,128)} %triangles.1) | copy-start | bytes 46084
  18.0 18.5 %collective-permute-start = (f32[43,8,128]{2,1,0:T(8,128)S(1)}, f32[43,8,128]{2,1,0:T(8,128)S(1)}, u32[]{:S(2)}, u32[]{:S(2)}) collective-permute-start(f32[43,8,128]{2,1,0:T(8,128)S(1)} %get-tuple-element.10), channel_id=1, source_target_pairs={{0,1},{1,2},{2,3},{4,5},{5,6},{6,7},{8,9},{9,10},{10,11},{12,13},{... | collective-permute-start | bytes 528392 | tf_op jit(solution)/shard_map/ppermute | solution.py:423
  27.2 12.7 %collective-permute-start.1 = (f32[43,8,128]{2,1,0:T(8,128)S(1)}, f32[43,8,128]{2,1,0:T(8,128)S(1)}, u32[]{:S(2)}, u32[]{:S(2)}) collective-permute-start(f32[43,8,128]{2,1,0:T(8,128)S(1)} %get-tuple-element.11), channel_id=1, source_target_pairs={{1,0},{2,1},{3,2},{5,4},{6,5},{7,6},{9,8},{10,9},{11,10},{13,12},{... | collective-permute-start | bytes 528392 | tf_op jit(solution)/shard_map/ppermute | solution.py:423
  36.5 3.5 %copy-start.7 = (f32[2,3,16,128]{3,2,1,0:T(8,128)}, f32[2,3,16,128]{3,2,1,0:T(8,128)S(1)}, u32[]{:S(2)}) copy-start(f32[2,3,16,128]{3,2,1,0:T(8,128)S(1)} %get-tuple-element.13) | copy-start | bytes 147460
  36.5 3.5 %copy-start.8 = (f32[2,3,16,128]{3,2,1,0:T(8,128)}, f32[2,3,16,128]{3,2,1,0:T(8,128)S(1)}, u32[]{:S(2)}) copy-start(f32[2,3,16,128]{3,2,1,0:T(8,128)S(1)} %get-tuple-element.12) | copy-start | bytes 147460
  40.0 22.3 %collective-permute-start.3 = (f32[110,16,128]{2,1,0:T(8,128)S(1)}, f32[110,16,128]{2,1,0:T(8,128)S(1)}, u32[]{:S(2)}, u32[]{:S(2)}) collective-permute-start(f32[110,16,128]{2,1,0:T(8,128)S(1)} %shard_map.99.own), channel_id=1, source_target_pairs={{4,0},{8,4},{12,8},{16,12},{20,16},{24,20},{28,24},{32,28},{36,32}... | collective-permute-start | bytes 2703368 | tf_op jit(solution)/shard_map/ppermute | solution.py:418
  46.6 20.6 %collective-permute-start.2 = (f32[110,16,128]{2,1,0:T(8,128)S(1)}, f32[110,16,128]{2,1,0:T(8,128)S(1)}, u32[]{:S(2)}, u32[]{:S(2)}) collective-permute-start(f32[110,16,128]{2,1,0:T(8,128)S(1)} %shard_map.99.own), channel_id=1, source_target_pairs={{0,4},{4,8},{8,12},{12,16},{16,20},{20,24},{24,28},{28,32},{32,36}... | collective-permute-start | bytes 2703368 | tf_op jit(solution)/shard_map/ppermute | solution.py:418
  48.6 12.5 %collective-permute-start.6 = (f32[128,8,128]{2,1,0:T(8,128)S(1)}, f32[128,8,128]{2,1,0:T(8,128)S(1)}, u32[]{:S(2)}, u32[]{:S(2)}) collective-permute-start(f32[128,8,128]{2,1,0:T(8,128)S(1)} %all-to-all-done), channel_id=1, source_target_pairs={{0,1},{1,0},{2,3},{3,2},{4,5},{5,4},{6,7},{7,6},{8,9},{9,8},{10,11... | collective-permute-start | bytes 1572872 | tf_op jit(solution)/shard_map/ppermute | solution.py:475
  50.5 18.8 %collective-permute-start.4 = (f32[2,3,16,128]{3,2,1,0:T(8,128)}, f32[2,3,16,128]{3,2,1,0:T(8,128)S(1)}, u32[]{:S(2)}, u32[]{:S(2)}) collective-permute-start(f32[2,3,16,128]{3,2,1,0:T(8,128)} %copy-done.8), channel_id=1, source_target_pairs={{0,8},{4,12},{8,16},{12,20},{16,24},{20,28},{24,32},{28,36},{32,40... | collective-permute-start | bytes 147464 | tf_op jit(solution)/shard_map/ppermute | solution.py:418
  52.4 16.9 %collective-permute-start.5 = (f32[2,3,16,128]{3,2,1,0:T(8,128)}, f32[2,3,16,128]{3,2,1,0:T(8,128)S(1)}, u32[]{:S(2)}, u32[]{:S(2)}) collective-permute-start(f32[2,3,16,128]{3,2,1,0:T(8,128)} %copy-done.7), channel_id=1, source_target_pairs={{8,0},{12,4},{16,8},{20,12},{24,16},{28,20},{32,24},{36,28},{40,32... | collective-permute-start | bytes 147464 | tf_op jit(solution)/shard_map/ppermute | solution.py:418

commit v3 on v2

--- a/solution.py
+++ b/solution.py
@@ -39,6 +39,9 @@
 DEEP = PLANES + 2 * STEPS
 WIDE = COLUMNS + 2 * STEPS
 CROSS = 4
+RISING = [q for q, c in enumerate(VELOCITIES) if c[0] == 1]
+FALLING = [q for q, c in enumerate(VELOCITIES) if c[0] == -1]
+FULL, FAR, RELAX, MASK, FORCE, TILES = 2, 59, 68, 72, 76, 91
 NODES = 768
 MEMBRANES = 16
 
@@ -74,7 +77,7 @@
         out[42, 0:3] = iface[...].astype(F32)
 
 
-def wide_kernel(pops, relax, mask, iface, force, from_left, from_right, wide_o):
+def wide_kernel(pops, relax, mask, iface, force, from_left, from_right, wide_o, up_o, down_o):
     for p in range(8):
         wide_o[86 + p * 3 : 89 + p * 3] = force[p]
     for z in range(PLANES):
@@ -94,6 +97,27 @@
     wide_o[84, 8:11] = iface[...].astype(F32)
     wide_o[85, 0:8] = from_right[42]
     wide_o[85, 8:16] = jnp.zeros((8, ROWS), F32)
+    for out, far, near, carried, first in ((up_o, 0, 1, RISING, 2), (down_o, 3, 0, FALLING, 5)):
+        out[0:FULL] = wide_o[84:86]
+        for q in range(19):
+            out[FULL + q * 3 : FULL + q * 3 + 3] = wide_o[q * 4 + near : q * 4 + near + 3]
+        fields = [wide_o[q * 4 + far] for q in range(19)]
+        fluid = wide_o[80 + far] > 0.5
+        for n, q in enumerate(carried):
+            out[FAR + n] = jnp.where(fluid, fields[q], fields[opposite(q)])
+        density, momentum = moments(fields)
+        inverse = 1.0 / wide_o[76 + far]
+        out[FAR + 5] = density
+        for d in range(3):
+            out[FAR + 6 + d] = momentum[d] + force[first, d] * inverse
+        out[RELAX:FORCE] = wide_o[76:84]
+        low = 3 if first == 2 else 0
+        for p in range(5):
+            out[FORCE + p * 3 : FORCE + p * 3 + 3] = force[low + p]
+
+
+def opposite(q):
+    return 0 if q == 0 else q + 1 if q % 2 else q - 1
 
 
 def nodal_kernel(positions, triangles, tension, out, x_s, table_s):
@@ -277,28 +301,37 @@
 def steps_kernel(
     own, up, down, force_m2, force_p2, found_own, found_far,
     pops_o, flow_o,
-    f_s, g_s, edge_s, hit_s, relax_s, mask_s, force_s,
+    f_s, g_s, edge_s, hit_s, force_s,
 ):
     j = lax.axis_index("slab")
     k = lax.axis_index("cross")
     slabs = lax.axis_size("slab")
-    for low, source in ((0, up), (4, own), (8, down)):
-        for q in range(19):
-            f_s[q, low + 1 : low + 5] = source[q * 4 : q * 4 + 4]
-        relax_s[low : low + 4] = source[76:80]
-        mask_s[low : low + 4] = source[80:84]
+
+    def tile(p, own_at, far_at):
+        part = p // 4
+        return own[own_at + p % 4] if part == 1 else (up, None, down)[part][far_at + p % 4]
+
+    def relaxation_of(p):
+        return tile(p, 76, RELAX)
+
+    def fluid_of(p):
+        return tile(p, 80, MASK) > 0.5
+
     for p in range(DEEP):
-        inverse = 1.0 / relax_s[p]
+        inverse = 1.0 / relaxation_of(p)
         for d in range(3):
-            value = None
-            for part, shift in ((own, -2), (up, 2), (down, -6)):
-                if 0 <= p + shift < 8:
-                    more = part[86 + (p + shift) * 3 + d]
-                    value = more if value is None else value + more
-            for part, low in ((force_m2, 0), (force_p2, 10)):
-                if low <= p < low + 2:
-                    value = value + part[p - low, d]
-            force_s[p, d] = value * inverse
+            parts = []
+            if 2 <= p < 10:
+                parts.append(own[86 + (p - 2) * 3 + d])
+            if 1 <= p < 6:
+                parts.append(up[FORCE + (p - 1) * 3 + d])
+            if 6 <= p < 11:
+                parts.append(down[FORCE + (p - 6) * 3 + d])
+            if p < 2:
+                parts.append(force_m2[p, d])
+            if p >= 10:
+                parts.append(force_p2[p - 10, d])
+            force_s[p, d] = sum(parts[1:], parts[0]) * inverse
 
     rows64 = lax.broadcasted_iota(I32, (64, 128), 0)
     rows128 = lax.broadcasted_iota(I32, (128, 128), 0)
@@ -313,7 +346,8 @@
             member = k + e
             there = slab_there & (member >= 0) & (member < CROSS)
             at = e + 1
-            cell = source[84 + at // 2, (at % 2) * 8 : (at % 2) * 8 + 1].astype(I32)
+            tile_at = (84 if d == 1 else 0) + at // 2
+            cell = source[tile_at, (at % 2) * 8 : (at % 2) * 8 + 1].astype(I32)
             amounts = found[found_at + at * 4 : found_at + at * 4 + 4]
             column = (cell >> 7) & 7
             if e == 0:
@@ -365,39 +399,53 @@
                 edge_s[2 * n + 1, p] = scaled * (even + along)
                 edge_s[2 * n + 2, p] = scaled * (even - along)
 
+    def collide(p, fields, density, momentum, wanted, put):
+        inverse = 1.0 / density
+        velocity = [(momentum[d] + force_s[p, d]) * inverse for d in range(3)]
+        omega = relaxation_of(p)
+        fluid = fluid_of(p)
+        keep = 1.0 - omega
+        amount = omega * density
+        base, pairs = equilibrium_terms(velocity)
+        if 0 in wanted:
+            put(0, jnp.where(fluid, keep * fields[0] + (amount * (1.0 / 3.0)) * base, fields[0]))
+        light = amount * (1.0 / 18.0)
+        lighter = amount * (1.0 / 36.0)
+        for n, (along, even) in enumerate(pairs):
+            scaled = light if n < 3 else lighter
+            for q in (2 * n + 1, 2 * n + 2):
+                if q in wanted:
+                    toward = even + along if q % 2 else even - along
+                    put(q, jnp.where(fluid, keep * fields[q] + scaled * toward, fields[opposite(q)]))
+
     for step in range(STEPS):
         source, dest = (f_s, g_s) if step % 2 == 0 else (g_s, f_s)
-
-        def plane(p, carry):
+        for p in range(step, DEEP - step):
+
+            def put(q, value, p=p, dest=dest):
+                c = VELOCITIES[q]
+                dest[q, p + 1 + c[0]] = rolled(value, c)
+
+            wanted = [q for q, c in enumerate(VELOCITIES) if step < p + c[0] < DEEP - 1 - step]
+            if step == 0 and p in (0, DEEP - 1):
+                message, carried = (up, RISING) if p == 0 else (down, FALLING)
+                fields = {}
+                for n, q in enumerate(carried):
+                    fields[q] = fields[opposite(q)] = message[FAR + n]
+                moved = [message[FAR + 6 + d] for d in range(3)]
+                collide(p, fields, message[FAR + 5], moved, wanted, put)
+                continue
             if step == 0:
-                fields = [source[q, p + 1] for q in range(19)]
+                if p // 4 == 1:
+                    fields = [own[q * 4 + p % 4] for q in range(19)]
+                else:
+                    message, near = (up, p - 1) if p < 4 else (down, p - 8)
+                    fields = [message[FULL + q * 3 + near] for q in range(19)]
             else:
                 hit = hit_s[p] > 0.5
                 fields = [jnp.where(hit, edge_s[q, p], source[q, p + 1]) for q in range(19)]
             density, momentum = moments(fields)
-            inverse = 1.0 / density
-            velocity = [(momentum[d] + force_s[p, d]) * inverse for d in range(3)]
-            omega = relax_s[p]
-            fluid = mask_s[p] > 0.5
-            keep = 1.0 - omega
-            amount = omega * density
-            base, pairs = equilibrium_terms(velocity)
-            dest[0, p + 1] = jnp.where(
-                fluid, keep * fields[0] + (amount * (1.0 / 3.0)) * base, fields[0]
-            )
-            light = amount * (1.0 / 18.0)
-            lighter = amount * (1.0 / 36.0)
-            for n, (along, even) in enumerate(pairs):
-                one, two = fields[2 * n + 1], fields[2 * n + 2]
-                scaled = light if n < 3 else lighter
-                c = VELOCITIES[2 * n + 1]
-                new_one = jnp.where(fluid, keep * one + scaled * (even + along), two)
-                new_two = jnp.where(fluid, keep * two + scaled * (even - along), one)
-                dest[2 * n + 1, p + 1 + c[0]] = rolled(new_one, c)
-                dest[2 * n + 2, p + 1 - c[0]] = rolled(new_two, tuple(-x for x in c))
-            return carry
-
-        lax.fori_loop(step, DEEP - step, plane, 0, unroll=2)
+            collide(p, fields, density, momentum, wanted, put)
 
     last = f_s if STEPS % 2 == 0 else g_s
     for z in range(PLANES):
@@ -467,14 +515,18 @@
         out_specs=tuple(whole_spec(n, 3, WIDE, ROWS) for n in counts),
         flops=1 << 31,
     )(nodes, partial)
-    wide = call(wide_kernel, struct(110, WIDE, ROWS))(*fields, force, from_left, from_right)
-    wide_up = slab_shift(wide, 1)
-    wide_down = slab_shift(wide, -1)
+    message = struct(TILES, WIDE, ROWS)
+    wide, for_up, for_down = call(wide_kernel, (struct(110, WIDE, ROWS), message, message))(
+        *fields, force, from_left, from_right
+    )
+    wide_up = slab_shift(for_up, 1)
+    wide_down = slab_shift(for_down, -1)
     force_m2 = slab_shift(to_up2, 2)
     force_p2 = slab_shift(to_down2, -2)
     other = lax.ppermute(table, "cross", [(s, s ^ 1) for s in range(CROSS)])
 
     tail = pl.BlockSpec((2, WIDE, ROWS), lambda i: (42, 0, 0))
+    head = pl.BlockSpec((2, WIDE, ROWS), lambda i: (0, 0, 0))
     found_own, lhs = call(
         lookup_own_kernel,
         (struct(12, ROWS), struct(4 * slabs, 1024, dtype=BF16)),
@@ -487,7 +539,7 @@
         lookup_far_kernel,
         struct(24, ROWS),
         grid=(1,),
-        in_specs=[whole_spec(4 * slabs, 1024), tail, tail],
+        in_specs=[whole_spec(4 * slabs, 1024), head, head],
         out_specs=whole_spec(24, ROWS),
         flops=1 << 30,
     )(lhs, wide_up, wide_down)
@@ -501,8 +553,6 @@
             state,
             state,
             pltpu.VMEM((19, DEEP, WIDE, ROWS), F32),
-            field,
-            field,
             field,
             pltpu.VMEM((DEEP, 3, WIDE, ROWS), F32),
         ],

time: 75.5 us -> 71.4 us (0.946)
  the two profiles are of different devices: /device:TPU:65 before, /device:TPU:118 now
where the time goes in v3:
time: 71.4 us; the launch traced here: 71 us
  starting transfers between devices  45.9 us (64%)
  Pallas kernels  16.7 us (23%)
  waiting for transfers between devices  6.88 us (10%)
  between operations  0.87 us (1%)
  local copies, waits for them, and re-layouts  0.72 us (1%)
    ppermute x4, starting transfers between devices, slab_shift(): return lax.ppermute(value, 'slab', pairs)  15.8 us
    all_to_all x1, starting transfers between devices, on_device(): lax.all_to_all(call(chunk_kernel, struct(slabs, 8, ROWS))(coarse_moments)...  15.7 us
    ppermute x1, starting transfers between devices, on_device(): other = lax.ppermute(table, 'cross', [(s, s ^ 1) for s in range(CROSS)])  11.6 us
    ppermute x4, waiting for transfers between devices, slab_shift(): return lax.ppermute(value, 'slab', pairs)  5.7 us
    pallas_call x1, Pallas kernels, on_device(): call(steps_kernel, (struct(*populations.shape), struct(3, *populations.sh...  3.82 us
    ppermute x2, starting transfers between devices, cross_shift(): return lax.ppermute(value, 'cross', pairs)  2.72 us
    pallas_call x1, Pallas kernels, on_device(): call(spread_first_kernel, struct(768, ROWS), grid=(1,), in_specs=[half_sp...  2.61 us
    pallas_call x1, Pallas kernels, on_device(): call(spread_last_kernel, tuple((struct(n, 3, WIDE, ROWS) for n in counts)...  2.61 us
  transfers between devices with their start and end apart: 8, of which 2 were waited for; matrix products, arithmetic and copies ran while one was open for 0% of the time, Pallas kernels for 17%

profile of v3, /device:TPU:118, one launch (start us, length us, event | category | flops | bytes accessed | tf_op | source)
XLA Modules:
  0.0 71.0 jit_solution(13289262420806789944)
XLA Ops:
  0.6 0.0 copy-start.3
  0.6 0.7 copy-done.3
  1.3 0.9 %shard_map.100 = f32[128,8,128]{2,1,0:T(8,128)} custom-call(f32[4,512]{1,0:T(4,128)S(1)} %copy-done.3), custom_call_target="tpu_custom_call" | custom-call | bytes 1048576 | tf_op jit(solution)/shard_map/pallas_call | solution.py:479
  2.2 0.0 copy-start
  2.2 0.0 copy-start.1
  2.2 0.0 copy-start.2
  2.2 0.0 copy-start.4
  2.2 15.7 %all-to-all-start = ((f32[128,8,128]{2,1,0:T(8,128)}), f32[128,8,128]{2,1,0:T(8,128)S(1)}, u32[]{:S(2)}, u32[]{:S(2)}) async-start(f32[128,8,128]{2,1,0:T(8,128)} %shard_map.100), calls=%async_computation | async-start | bytes 1048576 | tf_op jit(solution)/shard_map/all_to_all | solution.py:478
  17.9 0.0 copy-done
  17.9 0.0 copy-done.1
  17.9 0.0 copy-done.2
  17.9 0.0 copy-done.4
  17.9 0.0 copy-start.5
  17.9 0.0 copy-start.6
  17.9 0.0 copy-start.7
  18.0 1.4 %collective-permute-start = (f32[43,8,128]{2,1,0:T(8,128)S(1)}, f32[43,8,128]{2,1,0:T(8,128)S(1)}, u32[]{:S(2)}, u32[]{:S(2)}) collective-permute-start(f32[43,8,128]{2,1,0:T(8,128)S(1)} %get-tuple-element.13), channel_id=1, source_target_pairs={{0,1},{1,2},{2,3},{4,5},{5,6},{6,7},{8,9},{9,10},{10,11},{12,13},{... | collective-permute-start | bytes 528392 | tf_op jit(solution)/shard_map/ppermute | solution.py:471
  19.4 1.3 %collective-permute-start.1 = (f32[43,8,128]{2,1,0:T(8,128)S(1)}, f32[43,8,128]{2,1,0:T(8,128)S(1)}, u32[]{:S(2)}, u32[]{:S(2)}) collective-permute-start(f32[43,8,128]{2,1,0:T(8,128)S(1)} %get-tuple-element.14), channel_id=1, source_target_pairs={{1,0},{2,1},{3,2},{5,4},{6,5},{7,6},{9,8},{10,9},{11,10},{13,12},{... | collective-permute-start | bytes 528392 | tf_op jit(solution)/shard_map/ppermute | solution.py:471
  20.7 0.0 copy-done.5
  20.8 0.0 copy-done.6
  20.8 0.0 copy-done.7
  20.8 2.1 %shard_map.95.nodes = f32[16,8,768]{2,1,0:T(8,128)S(1)} custom-call(s32[3,16,642]{2,1,0:T(8,128)S(1)} %copy-done.5, s32[3,1280]{1,0:T(4,128)S(1)} %copy-done.7, f32[16,1280]{1,0:T(8,128)S(1)} %copy-done.6), custom_call_target="tpu_custom_call" | custom-call | flops 1073741824 | bytes 1048576 | tf_op jit(solution)/shard_map/pallas_call | solution.py:486
  22.9 2.6 %shard_map.96.partial = f32[768,128]{1,0:T(8,128)S(1)} custom-call(f32[16,8,768]{2,1,0:T(8,128)S(1)} %shard_map.95.nodes), custom_call_target="tpu_custom_call" | custom-call | flops 2147483648 | bytes 1048576 | tf_op jit(solution)/shard_map/pallas_call | solution.py:501
  25.5 2.6 %shard_map.97 = (f32[8,3,16,128]{3,2,1,0:T(8,128)S(1)}, f32[2,3,16,128]{3,2,1,0:T(8,128)S(1)}, f32[2,3,16,128]{3,2,1,0:T(8,128)S(1)}) custom-call(f32[16,8,768]{2,1,0:T(8,128)S(1)} %shard_map.95.nodes, f32[768,128]{1,0:T(8,128)S(1)} %shard_map.96.partial), custom_call_target="tpu_custom_call" | custom-call | flops 2147483648 | bytes 1048576 | tf_op jit(solution)/shard_map/pallas_call | solution.py:510
  28.1 0.0 collective-permute-done.from_left
  28.1 1.2 %collective-permute-done.1.from_right = f32[43,8,128]{2,1,0:T(8,128)S(1)} collective-permute-done((f32[43,8,128]{2,1,0:T(8,128)S(1)}, f32[43,8,128]{2,1,0:T(8,128)S(1)}, u32[]{:S(2)}, u32[]{:S(2)}) %collective-permute-start.1) | collective-permute-done | bytes 176160 | tf_op jit(solution)/shard_map/ppermute | solution.py:471
  29.3 1.4 %shard_map.99 = (f32[110,16,128]{2,1,0:T(8,128)S(1)}, f32[91,16,128]{2,1,0:T(8,128)}, f32[91,16,128]{2,1,0:T(8,128)}) custom-call(f32[19,4,8,128]{3,2,1,0:T(8,128)S(1)} %copy-done, f32[4,8,128]{2,1,0:T(8,128)S(1)} %copy-done.1, s32[4,8,128]{2,1,0:T(8,128)S(1)} %copy-done.2, s32[3,128]{1,0:T(4,128)S(1)} %copy-done.4, ...), custom_call_target="tpu_custom_call" | custom-call | bytes 1048576 | tf_op jit(solution)/shard_map/pallas_call | solution.py:519
  30.6 2.5 %collective-permute-start.2 = (f32[91,16,128]{2,1,0:T(8,128)}, f32[91,16,128]{2,1,0:T(8,128)S(1)}, u32[]{:S(2)}, u32[]{:S(2)}) collective-permute-start(f32[91,16,128]{2,1,0:T(8,128)} %get-tuple-element.16), channel_id=1, source_target_pairs={{0,4},{4,8},{8,12},{12,16},{16,20},{20,24},{24,28},{28,32},{32,36}... | collective-permute-start | bytes 2236424 | tf_op jit(solution)/shard_map/ppermute | solution.py:466
  33.1 3.4 %collective-permute-start.3 = (f32[91,16,128]{2,1,0:T(8,128)}, f32[91,16,128]{2,1,0:T(8,128)S(1)}, u32[]{:S(2)}, u32[]{:S(2)}) collective-permute-start(f32[91,16,128]{2,1,0:T(8,128)} %get-tuple-element.17), channel_id=1, source_target_pairs={{4,0},{8,4},{12,8},{16,12},{20,16},{24,20},{28,24},{32,28},{36,32}... | collective-permute-start | bytes 2236424 | tf_op jit(solution)/shard_map/ppermute | solution.py:466
  36.5 0.0 all-to-all-done
  36.5 11.6 %collective-permute-start.6 = (f32[128,8,128]{2,1,0:T(8,128)S(1)}, f32[128,8,128]{2,1,0:T(8,128)S(1)}, u32[]{:S(2)}, u32[]{:S(2)}) collective-permute-start(f32[128,8,128]{2,1,0:T(8,128)S(1)} %all-to-all-done), channel_id=1, source_target_pairs={{0,1},{1,0},{2,3},{3,2},{4,5},{5,4},{6,7},{7,6},{8,9},{9,8},{10,11... | collective-permute-start | bytes 1572872 | tf_op jit(solution)/shard_map/ppermute | solution.py:526
  48.2 7.9 %collective-permute-start.4 = (f32[2,3,16,128]{3,2,1,0:T(8,128)S(1)}, f32[2,3,16,128]{3,2,1,0:T(8,128)S(1)}, u32[]{:S(2)}, u32[]{:S(2)}) collective-permute-start(f32[2,3,16,128]{3,2,1,0:T(8,128)S(1)} %get-tuple-element.18), channel_id=1, source_target_pairs={{0,8},{4,12},{8,16},{12,20},{16,24},{20,28},{24,32},{28,36},{32,40... | collective-permute-start | bytes 147464 | tf_op jit(solution)/shard_map/ppermute | solution.py:466
  56.1 2.1 %collective-permute-start.5 = (f32[2,3,16,128]{3,2,1,0:T(8,128)S(1)}, f32[2,3,16,128]{3,2,1,0:T(8,128)S(1)}, u32[]{:S(2)}, u32[]{:S(2)}) collective-permute-start(f32[2,3,16,128]{3,2,1,0:T(8,128)S(1)} %get-tuple-element.19), channel_id=1, source_target_pairs={{8,0},{12,4},{16,8},{20,12},{24,16},{28,20},{32,24},{36,28},{40,32... | collective-permute-start | bytes 147464 | tf_op jit(solution)/shard_map/ppermute | solution.py:466
  58.2 0.0 collective-permute-done.6
  58.2 1.1 %shard_map.101 = (f32[12,128]{1,0:T(8,128)S(1)}, bf16[512,1024]{1,0:T(8,128)(2,1)S(1)}) custom-call(f32[1024,128]{1,0:T(8,128)S(1)} %bitcast.2, f32[1024,128]{1,0:T(8,128)S(1)} %bitcast.3, f32[110,16,128]{2,1,0:T(8,128)S(1)} %get-tuple-element.15.own), custom_call_target="tpu_custom_call" | custom-call | flops 1073741824 | bytes 1048576 | tf_op jit(solution)/shard_map/pallas_call | solution.py:530
  59.3 0.0 collective-permute-done.2.up
  59.3 0.0 collective-permute-done.3.down
  59.3 2.1 %shard_map.102.found_far = f32[24,128]{1,0:T(8,128)S(1)} custom-call(bf16[512,1024]{1,0:T(8,128)(2,1)S(1)} %get-tuple-element.21.lhs, f32[91,16,128]{2,1,0:T(8,128)S(1)} %collective-permute-done.2.up, f32[91,16,128]{2,1,0:T(8,128)S(1)} %collective-permute-done.3.down), custom_call_target="tpu_custom_call" | custom-call | flops 1073741824 | bytes 1048576 | tf_op jit(solution)/shard_map/pallas_call | solution.py:538
  61.5 0.0 collective-permute-done.4.force_m2
  61.5 5.7 %collective-permute-done.5.force_p2 = f32[2,3,16,128]{3,2,1,0:T(8,128)S(1)} collective-permute-done((f32[2,3,16,128]{3,2,1,0:T(8,128)S(1)}, f32[2,3,16,128]{3,2,1,0:T(8,128)S(1)}, u32[]{:S(2)}, u32[]{:S(2)}) %collective-permute-start.5) | collective-permute-done | bytes 49184 | tf_op jit(solution)/shard_map/ppermute | solution.py:466
  67.2 3.8 %shard_map.103 = (f32[19,4,8,128]{3,2,1,0:T(8,128)}, f32[3,4,8,128]{3,2,1,0:T(8,128)}) custom-call(f32[110,16,128]{2,1,0:T(8,128)S(1)} %get-tuple-element.15.own, f32[91,16,128]{2,1,0:T(8,128)S(1)} %collective-permute-done.2.up, f32[91,16,128]{2,1,0:T(8,128)S(1)} %collective-permute-done.3.down, f32[2,3,16,128]{3,2,1,0:T(8,128)S(1)} %collective-permute-done.4.force_m2, ...), custom_call_target="tpu_custom_call" | custom-call | flops 2147483648 | bytes 1048576 | tf_op jit(solution)/shard_map/pallas_call | solution.py:549
  (1 shorter events, 0.0 us)
Async XLA Ops:
  0.6 0.7 copy-start.3
  2.2 15.7 %copy-start = (f32[19,4,8,128]{3,2,1,0:T(8,128)S(1)}, f32[19,4,8,128]{3,2,1,0:T(8,128)}, u32[]{:S(2)}) copy-start(f32[19,4,8,128]{3,2,1,0:T(8,128)} %pops.3) | copy-start | bytes 933892
  2.2 15.7 %copy-start.1 = (f32[4,8,128]{2,1,0:T(8,128)S(1)}, f32[4,8,128]{2,1,0:T(8,128)}, u32[]{:S(2)}) copy-start(f32[4,8,128]{2,1,0:T(8,128)} %relax.3) | copy-start | bytes 49156
  2.2 15.7 %copy-start.2 = (s32[4,8,128]{2,1,0:T(8,128)S(1)}, s32[4,8,128]{2,1,0:T(8,128)}, u32[]{:S(2)}) copy-start(s32[4,8,128]{2,1,0:T(8,128)} %mask.3) | copy-start | bytes 49156
  2.2 15.7 %copy-start.4 = (s32[3,128]{1,0:T(4,128)S(1)}, s32[3,128]{1,0:T(4,128)}, u32[]{:S(2)}) copy-start(s32[3,128]{1,0:T(4,128)} %iface.3) | copy-start | bytes 4612
  2.2 34.3 %all-to-all-start = ((f32[128,8,128]{2,1,0:T(8,128)}), f32[128,8,128]{2,1,0:T(8,128)S(1)}, u32[]{:S(2)}, u32[]{:S(2)}) async-start(f32[128,8,128]{2,1,0:T(8,128)} %shard_map.100), calls=%async_computation | async-start | bytes 1048576 | tf_op jit(solution)/shard_map/all_to_all | solution.py:478
  17.9 2.8 %copy-start.5 = (s32[3,16,642]{2,1,0:T(8,128)S(1)}, s32[3,16,642]{2,1,0:T(8,128)}, u32[]{:S(2)}) copy-start(s32[3,16,642]{2,1,0:T(8,128)} %positions.1) | copy-start | bytes 369796
  17.9 2.8 %copy-start.6 = (f32[16,1280]{1,0:T(8,128)S(1)}, f32[16,1280]{1,0:T(8,128)}, u32[]{:S(2)}) copy-start(f32[16,1280]{1,0:T(8,128)} %tension.1) | copy-start | bytes 245764
  17.9 2.8 %copy-start.7 = (s32[3,1280]{1,0:T(4,128)S(1)}, s32[3,1280]{1,0:T(4,128)}, u32[]{:S(2)}) copy-start(s32[3,1280]{1,0:T(4,128)} %triangles.1) | copy-start | bytes 46084
  18.0 10.1 %collective-permute-start = (f32[43,8,128]{2,1,0:T(8,128)S(1)}, f32[43,8,128]{2,1,0:T(8,128)S(1)}, u32[]{:S(2)}, u32[]{:S(2)}) collective-permute-start(f32[43,8,128]{2,1,0:T(8,128)S(1)} %get-tuple-element.13), channel_id=1, source_target_pairs={{0,1},{1,2},{2,3},{4,5},{5,6},{6,7},{8,9},{9,10},{10,11},{12,13},{... | collective-permute-start | bytes 528392 | tf_op jit(solution)/shard_map/ppermute | solution.py:471
  19.4 9.8 %collective-permute-start.1 = (f32[43,8,128]{2,1,0:T(8,128)S(1)}, f32[43,8,128]{2,1,0:T(8,128)S(1)}, u32[]{:S(2)}, u32[]{:S(2)}) collective-permute-start(f32[43,8,128]{2,1,0:T(8,128)S(1)} %get-tuple-element.14), channel_id=1, source_target_pairs={{1,0},{2,1},{3,2},{5,4},{6,5},{7,6},{9,8},{10,9},{11,10},{13,12},{... | collective-permute-start | bytes 528392 | tf_op jit(solution)/shard_map/ppermute | solution.py:471
  30.6 28.7 %collective-permute-start.2 = (f32[91,16,128]{2,1,0:T(8,128)}, f32[91,16,128]{2,1,0:T(8,128)S(1)}, u32[]{:S(2)}, u32[]{:S(2)}) collective-permute-start(f32[91,16,128]{2,1,0:T(8,128)} %get-tuple-element.16), channel_id=1, source_target_pairs={{0,4},{4,8},{8,12},{12,16},{16,20},{20,24},{24,28},{28,32},{32,36}... | collective-permute-start | bytes 2236424 | tf_op jit(solution)/shard_map/ppermute | solution.py:466
  33.1 26.2 %collective-permute-start.3 = (f32[91,16,128]{2,1,0:T(8,128)}, f32[91,16,128]{2,1,0:T(8,128)S(1)}, u32[]{:S(2)}, u32[]{:S(2)}) collective-permute-start(f32[91,16,128]{2,1,0:T(8,128)} %get-tuple-element.17), channel_id=1, source_target_pairs={{4,0},{8,4},{12,8},{16,12},{20,16},{24,20},{28,24},{32,28},{36,32}... | collective-permute-start | bytes 2236424 | tf_op jit(solution)/shard_map/ppermute | solution.py:466
  36.5 21.7 %collective-permute-start.6 = (f32[128,8,128]{2,1,0:T(8,128)S(1)}, f32[128,8,128]{2,1,0:T(8,128)S(1)}, u32[]{:S(2)}, u32[]{:S(2)}) collective-permute-start(f32[128,8,128]{2,1,0:T(8,128)S(1)} %all-to-all-done), channel_id=1, source_target_pairs={{0,1},{1,0},{2,3},{3,2},{4,5},{5,4},{6,7},{7,6},{8,9},{9,8},{10,11... | collective-permute-start | bytes 1572872 | tf_op jit(solution)/shard_map/ppermute | solution.py:526
  48.2 13.3 %collective-permute-start.4 = (f32[2,3,16,128]{3,2,1,0:T(8,128)S(1)}, f32[2,3,16,128]{3,2,1,0:T(8,128)S(1)}, u32[]{:S(2)}, u32[]{:S(2)}) collective-permute-start(f32[2,3,16,128]{3,2,1,0:T(8,128)S(1)} %get-tuple-element.18), channel_id=1, source_target_pairs={{0,8},{4,12},{8,16},{12,20},{16,24},{20,28},{24,32},{28,36},{32,40... | collective-permute-start | bytes 147464 | tf_op jit(solution)/shard_map/ppermute | solution.py:466
  56.1 11.1 %collective-permute-start.5 = (f32[2,3,16,128]{3,2,1,0:T(8,128)S(1)}, f32[2,3,16,128]{3,2,1,0:T(8,128)S(1)}, u32[]{:S(2)}, u32[]{:S(2)}) collective-permute-start(f32[2,3,16,128]{3,2,1,0:T(8,128)S(1)} %get-tuple-element.19), channel_id=1, source_target_pairs={{8,0},{12,4},{16,8},{20,12},{24,16},{28,20},{32,24},{36,28},{40,32... | collective-permute-start | bytes 147464 | tf_op jit(solution)/shard_map/ppermute | solution.py:466

commit v4 on v3

--- a/solution.py
+++ b/solution.py
@@ -61,42 +61,54 @@
     return jax.ShapeDtypeStruct(shape, dtype)
 
 
-def pack_kernel(pops, relax, mask, iface, right_o, left_o):
+def on_even_member():
+    return lax.rem(lax.axis_index("cross"), 2) == 0
+
+
+def pack_kernel(pops, relax, mask, iface, core_o, chip_o):
+    even = on_even_member()
+
     def put(field, z, value):
         low = (z % 2) * 4
-        right_o[field * 2 + z // 2, low : low + 4] = value[4:8]
-        left_o[field * 2 + z // 2, low : low + 4] = value[0:4]
+        core_o[field * 2 + z // 2, low : low + 4] = jnp.where(even, value[4:8], value[0:4])
+        chip_o[field * 2 + z // 2, low : low + 4] = jnp.where(even, value[0:4], value[4:8])
 
     for z in range(PLANES):
         for q in range(19):
             put(q, z, pops[q, z])
         put(19, z, relax[z])
         put(20, z, mask[z].astype(F32))
-    for out in (right_o, left_o):
+    for out in (core_o, chip_o):
         out[42] = jnp.zeros((8, ROWS), F32)
         out[42, 0:3] = iface[...].astype(F32)
 
 
-def wide_kernel(pops, relax, mask, iface, force, from_left, from_right, wide_o, up_o, down_o):
-    for p in range(8):
-        wide_o[86 + p * 3 : 89 + p * 3] = force[p]
+def wide_kernel(pops, relax, mask, iface, force, from_core, from_chip, up_o, down_o, first_o, wide_o):
     for z in range(PLANES):
         for q in range(19):
             wide_o[q * 4 + z, 0:8] = pops[q, z]
         wide_o[76 + z, 0:8] = relax[z]
         wide_o[80 + z, 0:8] = mask[z].astype(F32)
+    even = on_even_member()
+
+    def sides(tile):
+        one, two = from_core[tile], from_chip[tile]
+        return jnp.where(even, two, one), jnp.where(even, one, two)
+
     for tile in range(42):
-        right = from_right[tile]
-        left = from_left[tile]
+        left, right = sides(tile)
         wide_o[2 * tile, 8:12] = right[0:4]
         wide_o[2 * tile + 1, 8:12] = right[4:8]
         wide_o[2 * tile, 12:16] = left[0:4]
         wide_o[2 * tile + 1, 12:16] = left[4:8]
-    wide_o[84, 0:8] = from_left[42]
+    left, right = sides(42)
+    wide_o[84, 0:8] = left
     wide_o[84, 8:16] = jnp.zeros((8, ROWS), F32)
     wide_o[84, 8:11] = iface[...].astype(F32)
-    wide_o[85, 0:8] = from_right[42]
+    wide_o[85, 0:8] = right
     wide_o[85, 8:16] = jnp.zeros((8, ROWS), F32)
+    for q in range(19):
+        first_o[q] = wide_o[q * 4]
     for out, far, near, carried, first in ((up_o, 0, 1, RISING, 2), (down_o, 3, 0, FALLING, 5)):
         out[0:FULL] = wide_o[84:86]
         for q in range(19):
@@ -154,7 +166,7 @@
             out[m, 3 + d : 4 + d, 0:642] = place[m : m + 1]
 
 
-def spread_body(nodes, initial, finished):
+def spread_body(nodes):
     plane_ids = lax.broadcasted_iota(I32, (8, NODES), 0).astype(F32) - 2.0
     column_ids = lax.broadcasted_iota(I32, (WIDE, NODES), 0)
     column_ids = jnp.where(column_ids < 12, column_ids, column_ids - 16).astype(F32)
@@ -184,15 +196,12 @@
             lhs, along_row, (((1,), (1,)), ((), ())), preferred_element_type=F32
         )
 
+    initial = jnp.zeros((768, ROWS), F32)
     return lax.fori_loop(0, nodes.shape[0], add, initial, unroll=True)
 
 
-def spread_first_kernel(nodes, out):
-    out[...] = spread_body(nodes, jnp.zeros((768, ROWS), F32), None)
-
-
-def spread_last_kernel(nodes, partial, own_o, up2_o, down2_o):
-    total = spread_body(nodes, partial[...], None)
+def spread_kernel(nodes, own_o, up2_o, down2_o):
+    total = spread_body(nodes)
     for p in range(8):
         for d in range(3):
             low = p * 96 + d * 16
@@ -299,7 +308,7 @@
 
 
 def steps_kernel(
-    own, up, down, force_m2, force_p2, found_own, found_far,
+    own_up, first_plane, up, down, force, force_m2, force_p2, found_own, found_far,
     pops_o, flow_o,
     f_s, g_s, edge_s, hit_s, force_s,
 ):
@@ -307,22 +316,21 @@
     k = lax.axis_index("cross")
     slabs = lax.axis_size("slab")
 
-    def tile(p, own_at, far_at):
-        part = p // 4
-        return own[own_at + p % 4] if part == 1 else (up, None, down)[part][far_at + p % 4]
+    def tile(p, at):
+        return (up, own_up, down)[p // 4][at + p % 4]
 
     def relaxation_of(p):
-        return tile(p, 76, RELAX)
+        return tile(p, RELAX)
 
     def fluid_of(p):
-        return tile(p, 80, MASK) > 0.5
+        return tile(p, MASK) > 0.5
 
     for p in range(DEEP):
         inverse = 1.0 / relaxation_of(p)
         for d in range(3):
             parts = []
             if 2 <= p < 10:
-                parts.append(own[86 + (p - 2) * 3 + d])
+                parts.append(force[p - 2, d])
             if 1 <= p < 6:
                 parts.append(up[FORCE + (p - 1) * 3 + d])
             if 6 <= p < 11:
@@ -337,7 +345,7 @@
     rows128 = lax.broadcasted_iota(I32, (128, 128), 0)
     ids = lax.broadcasted_iota(I32, (WIDE, ROWS), 0)
     founds = ((found_far, 0), (found_own, 0), (found_far, 12))
-    for d, source in enumerate((up, own, down)):
+    for d, source in enumerate((up, own_up, down)):
         found, found_at = founds[d]
         slab_there = (j + d - 1 >= 0) & (j + d - 1 < slabs)
         lhs = []
@@ -346,8 +354,7 @@
             member = k + e
             there = slab_there & (member >= 0) & (member < CROSS)
             at = e + 1
-            tile_at = (84 if d == 1 else 0) + at // 2
-            cell = source[tile_at, (at % 2) * 8 : (at % 2) * 8 + 1].astype(I32)
+            cell = source[at // 2, (at % 2) * 8 : (at % 2) * 8 + 1].astype(I32)
             amounts = found[found_at + at * 4 : found_at + at * 4 + 4]
             column = (cell >> 7) & 7
             if e == 0:
@@ -436,10 +443,15 @@
                 collide(p, fields, message[FAR + 5], moved, wanted, put)
                 continue
             if step == 0:
-                if p // 4 == 1:
-                    fields = [own[q * 4 + p % 4] for q in range(19)]
+                if p < 4:
+                    message, near = up, p - 1
+                elif p < 8:
+                    message, near = own_up, p - 5
                 else:
-                    message, near = (up, p - 1) if p < 4 else (down, p - 8)
+                    message, near = down, p - 8
+                if p == 4:
+                    fields = [first_plane[q] for q in range(19)]
+                else:
                     fields = [message[FULL + q * 3 + near] for q in range(19)]
             else:
                 hit = hit_s[p] > 0.5
@@ -466,8 +478,10 @@
     return lax.ppermute(value, "slab", pairs)
 
 
-def cross_shift(value, steps):
-    pairs = [(s, s + steps) for s in range(CROSS) if 0 <= s + steps < CROSS]
+def cross_swap(value, first):
+    pairs = []
+    for s in range(first, CROSS - 1, 2):
+        pairs += [(s, s + 1), (s + 1, s)]
     return lax.ppermute(value, "cross", pairs)
 
 
@@ -480,9 +494,9 @@
     )
 
     fields = (populations, relaxation, fluid_mask, interface)
-    to_right, to_left = call(pack_kernel, (struct(43, 8, ROWS), struct(43, 8, ROWS)))(*fields)
-    from_left = cross_shift(to_right, 1)
-    from_right = cross_shift(to_left, -1)
+    to_core, to_chip = call(pack_kernel, (struct(43, 8, ROWS), struct(43, 8, ROWS)))(*fields)
+    from_core = cross_swap(to_core, 0)
+    from_chip = cross_swap(to_chip, 1)
     nodes = call(
         nodal_kernel,
         struct(MEMBRANES, 8, NODES),
@@ -490,51 +504,37 @@
         flops=1 << 30,
     )(positions, triangles, tension)
 
-    half = MEMBRANES // 2
-
-    def half_spec(at):
-        return pl.BlockSpec((half, 8, NODES), lambda i: (at, 0, 0))
-
     def whole_spec(*shape):
         return pl.BlockSpec(shape, lambda i: (0,) * len(shape))
 
-    partial = call(
-        spread_first_kernel,
-        struct(768, ROWS),
+    counts = (8, 2, 2)
+    force, to_up2, to_down2 = call(
+        spread_kernel,
+        tuple(struct(n, 3, WIDE, ROWS) for n in counts),
         grid=(1,),
-        in_specs=[half_spec(0)],
-        out_specs=whole_spec(768, ROWS),
+        in_specs=[whole_spec(MEMBRANES, 8, NODES)],
+        out_specs=tuple(whole_spec(n, 3, WIDE, ROWS) for n in counts),
         flops=1 << 31,
     )(nodes)
-    counts = (8, 2, 2)
-    force, to_up2, to_down2 = call(
-        spread_last_kernel,
-        tuple(struct(n, 3, WIDE, ROWS) for n in counts),
-        grid=(1,),
-        in_specs=[half_spec(1), whole_spec(768, ROWS)],
-        out_specs=tuple(whole_spec(n, 3, WIDE, ROWS) for n in counts),
-        flops=1 << 31,
-    )(nodes, partial)
     message = struct(TILES, WIDE, ROWS)
-    wide, for_up, for_down = call(wide_kernel, (struct(110, WIDE, ROWS), message, message))(
-        *fields, force, from_left, from_right
-    )
+    for_up, for_down, first_plane = call(
+        wide_kernel, (message, message, struct(19, WIDE, ROWS)), [pltpu.VMEM((86, WIDE, ROWS), F32)]
+    )(*fields, force, from_core, from_chip)
     wide_up = slab_shift(for_up, 1)
     wide_down = slab_shift(for_down, -1)
     force_m2 = slab_shift(to_up2, 2)
     force_p2 = slab_shift(to_down2, -2)
-    other = lax.ppermute(table, "cross", [(s, s ^ 1) for s in range(CROSS)])
-
-    tail = pl.BlockSpec((2, WIDE, ROWS), lambda i: (42, 0, 0))
+    other = cross_swap(table, 0)
+
     head = pl.BlockSpec((2, WIDE, ROWS), lambda i: (0, 0, 0))
     found_own, lhs = call(
         lookup_own_kernel,
         (struct(12, ROWS), struct(4 * slabs, 1024, dtype=BF16)),
         grid=(1,),
-        in_specs=[whole_spec(slabs * 8, ROWS), whole_spec(slabs * 8, ROWS), tail],
+        in_specs=[whole_spec(slabs * 8, ROWS), whole_spec(slabs * 8, ROWS), head],
         out_specs=(whole_spec(12, ROWS), whole_spec(4 * slabs, 1024)),
         flops=1 << 30,
-    )(table.reshape(slabs * 8, ROWS), other.reshape(slabs * 8, ROWS), wide)
+    )(table.reshape(slabs * 8, ROWS), other.reshape(slabs * 8, ROWS), for_up)
     found_far = call(
         lookup_far_kernel,
         struct(24, ROWS),
@@ -558,7 +558,7 @@
         ],
         flops=1 << 31,
     )(
-        wide, wide_up, wide_down, force_m2, force_p2, found_own, found_far
+        for_up, first_plane, wide_up, wide_down, force, force_m2, force_p2, found_own, found_far
     )
 
 

time: 71.4 us -> 69.8 us (0.978)
  the two profiles are of different devices: /device:TPU:118 before, /device:TPU:65 now
where the time goes in v4:
time: 69.8 us; the launch traced here: 69.4 us
  starting transfers between devices  47.5 us (68%)
  Pallas kernels  16.1 us (23%)
  waiting for transfers between devices  4.16 us (6%)
  between operations  0.88 us (1%)
  local copies, waits for them, and re-layouts  0.73 us (1%)
    ppermute x4, starting transfers between devices, slab_shift(): return lax.ppermute(value, 'slab', pairs)  18.8 us
    all_to_all x1, starting transfers between devices, on_device(): lax.all_to_all(call(chunk_kernel, struct(slabs, 8, ROWS))(coarse_moments)...  15.7 us
    ppermute x3, starting transfers between devices, cross_swap(): return lax.ppermute(value, 'cross', pairs)  13 us
    pallas_call x1, Pallas kernels, on_device(): call(spread_kernel, tuple((struct(n, 3, WIDE, ROWS) for n in counts)), gr...  5.03 us
    pallas_call x1, Pallas kernels, on_device(): call(steps_kernel, (struct(*populations.shape), struct(3, *populations.sh...  3.78 us
    ppermute x4, waiting for transfers between devices, slab_shift(): return lax.ppermute(value, 'slab', pairs)  3.32 us
    pallas_call x1, Pallas kernels, on_device(): call(lookup_far_kernel, struct(24, ROWS), grid=(1,), in_specs=[whole_spec...  2.1 us
    pallas_call x1, Pallas kernels, on_device(): call(nodal_kernel, struct(MEMBRANES, 8, NODES), [pltpu.VMEM((48, NODES),...  2.1 us
  transfers between devices with their start and end apart: 8, of which 2 were waited for; matrix products, arithmetic and copies ran while one was open for 0% of the time, Pallas kernels for 17%

profile of v4, /device:TPU:65, one launch (start us, length us, event | category | flops | bytes accessed | tf_op | source)
XLA Modules:
  0.0 69.4 jit_solution(8043901753686877904)
XLA Ops:
  0.6 0.0 copy-start.3
  0.6 0.7 copy-done.3
  1.3 0.8 %shard_map.99 = f32[128,8,128]{2,1,0:T(8,128)} custom-call(f32[4,512]{1,0:T(4,128)S(1)} %copy-done.3), custom_call_target="tpu_custom_call" | custom-call | bytes 1048576 | tf_op jit(solution)/shard_map/pallas_call | solution.py:493
  2.2 0.0 copy-start
  2.2 0.0 copy-start.1
  2.2 0.0 copy-start.2
  2.2 0.0 copy-start.4
  2.2 15.7 %all-to-all-start = ((f32[128,8,128]{2,1,0:T(8,128)}), f32[128,8,128]{2,1,0:T(8,128)S(1)}, u32[]{:S(2)}, u32[]{:S(2)}) async-start(f32[128,8,128]{2,1,0:T(8,128)} %shard_map.99), calls=%async_computation | async-start | bytes 1048576 | tf_op jit(solution)/shard_map/all_to_all | solution.py:492
  17.9 0.0 copy-done
  17.9 0.0 copy-done.1
  17.9 0.0 copy-done.2
  17.9 0.0 copy-done.4
  17.9 0.0 copy-start.5
  17.9 0.0 copy-start.6
  17.9 0.0 copy-start.8
  17.9 0.1 shard_map.97
  18.0 3.3 %collective-permute-start = (f32[43,8,128]{2,1,0:T(8,128)S(1)}, f32[43,8,128]{2,1,0:T(8,128)S(1)}, u32[]{:S(2)}, u32[]{:S(2)}) collective-permute-start(f32[43,8,128]{2,1,0:T(8,128)S(1)} %get-tuple-element.13), channel_id=1, source_target_pairs={{0,1},{1,0},{2,3},{3,2},{4,5},{5,4},{6,7},{7,6},{8,9},{9,8},{10,11... | collective-permute-start | bytes 528392 | tf_op jit(solution)/shard_map/ppermute | solution.py:485
  21.3 7.8 %collective-permute-start.1 = (f32[43,8,128]{2,1,0:T(8,128)S(1)}, f32[43,8,128]{2,1,0:T(8,128)S(1)}, u32[]{:S(2)}, u32[]{:S(2)}) collective-permute-start(f32[43,8,128]{2,1,0:T(8,128)S(1)} %get-tuple-element.14), channel_id=1, source_target_pairs={{1,2},{2,1},{5,6},{6,5},{9,10},{10,9},{13,14},{14,13},{17,18},{18,... | collective-permute-start | bytes 528392 | tf_op jit(solution)/shard_map/ppermute | solution.py:485
  29.1 0.0 copy-done.5
  29.1 0.0 copy-done.6
  29.1 0.0 copy-done.8
  29.2 2.1 %shard_map.95.nodes = f32[16,8,768]{2,1,0:T(8,128)S(1)} custom-call(s32[3,16,642]{2,1,0:T(8,128)S(1)} %copy-done.5, s32[3,1280]{1,0:T(4,128)S(1)} %copy-done.8, f32[16,1280]{1,0:T(8,128)S(1)} %copy-done.6), custom_call_target="tpu_custom_call" | custom-call | flops 1073741824 | bytes 1048576 | tf_op jit(solution)/shard_map/pallas_call | solution.py:500
  31.3 5.0 %shard_map.96 = (f32[8,3,16,128]{3,2,1,0:T(8,128)S(1)}, f32[2,3,16,128]{3,2,1,0:T(8,128)S(1)}, f32[2,3,16,128]{3,2,1,0:T(8,128)S(1)}) custom-call(f32[16,8,768]{2,1,0:T(8,128)S(1)} %shard_map.95.nodes), custom_call_target="tpu_custom_call" | custom-call | flops 2147483648 | bytes 1048576 | tf_op jit(solution)/shard_map/pallas_call | solution.py:511
  36.3 0.0 copy-start.7
  36.3 0.0 collective-permute-done.from_core
  36.3 0.8 %collective-permute-done.1.from_chip = f32[43,8,128]{2,1,0:T(8,128)S(1)} collective-permute-done((f32[43,8,128]{2,1,0:T(8,128)S(1)}, f32[43,8,128]{2,1,0:T(8,128)S(1)}, u32[]{:S(2)}, u32[]{:S(2)}) %collective-permute-start.1) | collective-permute-done | bytes 176160 | tf_op jit(solution)/shard_map/ppermute | solution.py:485
  37.2 1.0 %shard_map.98 = (f32[91,16,128]{2,1,0:T(8,128)S(1)}, f32[91,16,128]{2,1,0:T(8,128)}, f32[19,16,128]{2,1,0:T(8,128)S(1)}) custom-call(f32[19,4,8,128]{3,2,1,0:T(8,128)S(1)} %copy-done, f32[4,8,128]{2,1,0:T(8,128)S(1)} %copy-done.1, s32[4,8,128]{2,1,0:T(8,128)S(1)} %copy-done.2, s32[3,128]{1,0:T(4,128)S(1)} %copy-done.4, ...), custom_call_target="tpu_custom_call" | custom-call | bytes 1048576 | tf_op jit(solution)/shard_map/pallas_call | solution.py:520
  38.2 0.0 copy-done.7
  38.2 6.3 %collective-permute-start.3 = (f32[91,16,128]{2,1,0:T(8,128)}, f32[91,16,128]{2,1,0:T(8,128)S(1)}, u32[]{:S(2)}, u32[]{:S(2)}) collective-permute-start(f32[91,16,128]{2,1,0:T(8,128)} %get-tuple-element.17), channel_id=1, source_target_pairs={{4,0},{8,4},{12,8},{16,12},{20,16},{24,20},{28,24},{32,28},{36,32}... | collective-permute-start | bytes 2236424 | tf_op jit(solution)/shard_map/ppermute | solution.py:478
  44.5 1.9 %collective-permute-start.2 = (f32[91,16,128]{2,1,0:T(8,128)S(1)}, f32[91,16,128]{2,1,0:T(8,128)S(1)}, u32[]{:S(2)}, u32[]{:S(2)}) collective-permute-start(f32[91,16,128]{2,1,0:T(8,128)S(1)} %get-tuple-element.15.own.own_up), channel_id=1, source_target_pairs={{0,4},{4,8},{8,12},{12,16},{16,20},{20,24},{24,28},{28,32},{32,36}... | collective-permute-start | bytes 2236424 | tf_op jit(solution)/shard_map/ppermute | solution.py:478
  46.5 0.0 all-to-all-done
  46.5 1.9 %collective-permute-start.6 = (f32[128,8,128]{2,1,0:T(8,128)S(1)}, f32[128,8,128]{2,1,0:T(8,128)S(1)}, u32[]{:S(2)}, u32[]{:S(2)}) collective-permute-start(f32[128,8,128]{2,1,0:T(8,128)S(1)} %all-to-all-done), channel_id=1, source_target_pairs={{0,1},{1,0},{2,3},{3,2},{4,5},{5,4},{6,7},{7,6},{8,9},{9,8},{10,11... | collective-permute-start | bytes 1572872 | tf_op jit(solution)/shard_map/ppermute | solution.py:485
  48.4 1.9 %collective-permute-start.4 = (f32[2,3,16,128]{3,2,1,0:T(8,128)}, f32[2,3,16,128]{3,2,1,0:T(8,128)S(1)}, u32[]{:S(2)}, u32[]{:S(2)}) collective-permute-start(f32[2,3,16,128]{3,2,1,0:T(8,128)} %copy-done.7), channel_id=1, source_target_pairs={{0,8},{4,12},{8,16},{12,20},{16,24},{20,28},{24,32},{28,36},{32,40... | collective-permute-start | bytes 147464 | tf_op jit(solution)/shard_map/ppermute | solution.py:478
  50.3 8.7 %collective-permute-start.5 = (f32[2,3,16,128]{3,2,1,0:T(8,128)S(1)}, f32[2,3,16,128]{3,2,1,0:T(8,128)S(1)}, u32[]{:S(2)}, u32[]{:S(2)}) collective-permute-start(f32[2,3,16,128]{3,2,1,0:T(8,128)S(1)} %get-tuple-element.19), channel_id=1, source_target_pairs={{8,0},{12,4},{16,8},{20,12},{24,16},{28,20},{32,24},{36,28},{40,32... | collective-permute-start | bytes 147464 | tf_op jit(solution)/shard_map/ppermute | solution.py:478
  59.0 0.0 collective-permute-done.6
  59.0 1.1 %shard_map.100 = (f32[12,128]{1,0:T(8,128)S(1)}, bf16[512,1024]{1,0:T(8,128)(2,1)S(1)}) custom-call(f32[1024,128]{1,0:T(8,128)S(1)} %bitcast.2, f32[1024,128]{1,0:T(8,128)S(1)} %bitcast.3, f32[91,16,128]{2,1,0:T(8,128)S(1)} %get-tuple-element.15.own.own_up), custom_call_target="tpu_custom_call" | custom-call | flops 1073741824 | bytes 1048576 | tf_op jit(solution)/shard_map/pallas_call | solution.py:530
  60.1 0.0 collective-permute-done.3.down
  60.1 3.3 %collective-permute-done.2.up = f32[91,16,128]{2,1,0:T(8,128)S(1)} collective-permute-done((f32[91,16,128]{2,1,0:T(8,128)S(1)}, f32[91,16,128]{2,1,0:T(8,128)S(1)}, u32[]{:S(2)}, u32[]{:S(2)}) %collective-permute-start.2) | collective-permute-done | bytes 745504 | tf_op jit(solution)/shard_map/ppermute | solution.py:478
  63.5 2.1 %shard_map.101.found_far = f32[24,128]{1,0:T(8,128)S(1)} custom-call(bf16[512,1024]{1,0:T(8,128)(2,1)S(1)} %get-tuple-element.21.lhs, f32[91,16,128]{2,1,0:T(8,128)S(1)} %collective-permute-done.2.up, f32[91,16,128]{2,1,0:T(8,128)S(1)} %collective-permute-done.3.down), custom_call_target="tpu_custom_call" | custom-call | flops 1073741824 | bytes 1048576 | tf_op jit(solution)/shard_map/pallas_call | solution.py:538
  65.6 0.0 collective-permute-done.4.force_m2
  65.6 0.0 collective-permute-done.5.force_p2
  65.6 3.8 %shard_map.102 = (f32[19,4,8,128]{3,2,1,0:T(8,128)}, f32[3,4,8,128]{3,2,1,0:T(8,128)}) custom-call(f32[91,16,128]{2,1,0:T(8,128)S(1)} %get-tuple-element.15.own.own_up, f32[19,16,128]{2,1,0:T(8,128)S(1)} %get-tuple-element.16.first_plane, f32[91,16,128]{2,1,0:T(8,128)S(1)} %collective-permute-done.2.up, f32[91,16,128]{2,1,0:T(8,128)S(1)} %collective-permute-done.3.down, ...), custom_call_target="tpu_custom_call" | custom-call | flops 2147483648 | bytes 1048576 | tf_op jit(solution)/shard_map/pallas_call | solution.py:549
Async XLA Ops:
  0.6 0.7 %copy-start.3 = (f32[4,512]{1,0:T(4,128)S(1)}, f32[4,512]{1,0:T(4,128)}, u32[]{:S(2)}) copy-start(f32[4,512]{1,0:T(4,128)} %coarse.1) | copy-start | bytes 24580
  2.2 15.7 %copy-start = (f32[19,4,8,128]{3,2,1,0:T(8,128)S(1)}, f32[19,4,8,128]{3,2,1,0:T(8,128)}, u32[]{:S(2)}) copy-start(f32[19,4,8,128]{3,2,1,0:T(8,128)} %pops.3) | copy-start | bytes 933892
  2.2 15.7 %copy-start.1 = (f32[4,8,128]{2,1,0:T(8,128)S(1)}, f32[4,8,128]{2,1,0:T(8,128)}, u32[]{:S(2)}) copy-start(f32[4,8,128]{2,1,0:T(8,128)} %relax.3) | copy-start | bytes 49156
  2.2 15.7 %copy-start.2 = (s32[4,8,128]{2,1,0:T(8,128)S(1)}, s32[4,8,128]{2,1,0:T(8,128)}, u32[]{:S(2)}) copy-start(s32[4,8,128]{2,1,0:T(8,128)} %mask.3) | copy-start | bytes 49156
  2.2 15.7 %copy-start.4 = (s32[3,128]{1,0:T(4,128)S(1)}, s32[3,128]{1,0:T(4,128)}, u32[]{:S(2)}) copy-start(s32[3,128]{1,0:T(4,128)} %iface.3) | copy-start | bytes 4612
  2.2 44.3 %all-to-all-start = ((f32[128,8,128]{2,1,0:T(8,128)}), f32[128,8,128]{2,1,0:T(8,128)S(1)}, u32[]{:S(2)}, u32[]{:S(2)}) async-start(f32[128,8,128]{2,1,0:T(8,128)} %shard_map.99), calls=%async_computation | async-start | bytes 1048576 | tf_op jit(solution)/shard_map/all_to_all | solution.py:492
  17.9 11.2 %copy-start.5 = (s32[3,16,642]{2,1,0:T(8,128)S(1)}, s32[3,16,642]{2,1,0:T(8,128)}, u32[]{:S(2)}) copy-start(s32[3,16,642]{2,1,0:T(8,128)} %positions.1) | copy-start | bytes 369796
  17.9 11.2 %copy-start.6 = (f32[16,1280]{1,0:T(8,128)S(1)}, f32[16,1280]{1,0:T(8,128)}, u32[]{:S(2)}) copy-start(f32[16,1280]{1,0:T(8,128)} %tension.1) | copy-start | bytes 245764
  17.9 11.2 %copy-start.8 = (s32[3,1280]{1,0:T(4,128)S(1)}, s32[3,1280]{1,0:T(4,128)}, u32[]{:S(2)}) copy-start(s32[3,1280]{1,0:T(4,128)} %triangles.1) | copy-start | bytes 46084
  18.0 18.3 %collective-permute-start = (f32[43,8,128]{2,1,0:T(8,128)S(1)}, f32[43,8,128]{2,1,0:T(8,128)S(1)}, u32[]{:S(2)}, u32[]{:S(2)}) collective-permute-start(f32[43,8,128]{2,1,0:T(8,128)S(1)} %get-tuple-element.13), channel_id=1, source_target_pairs={{0,1},{1,0},{2,3},{3,2},{4,5},{5,4},{6,7},{7,6},{8,9},{9,8},{10,11... | collective-permute-start | bytes 528392 | tf_op jit(solution)/shard_map/ppermute | solution.py:485
  21.3 15.9 %collective-permute-start.1 = (f32[43,8,128]{2,1,0:T(8,128)S(1)}, f32[43,8,128]{2,1,0:T(8,128)S(1)}, u32[]{:S(2)}, u32[]{:S(2)}) collective-permute-start(f32[43,8,128]{2,1,0:T(8,128)S(1)} %get-tuple-element.14), channel_id=1, source_target_pairs={{1,2},{2,1},{5,6},{6,5},{9,10},{10,9},{13,14},{14,13},{17,18},{18,... | collective-permute-start | bytes 528392 | tf_op jit(solution)/shard_map/ppermute | solution.py:485
  36.3 1.9 %copy-start.7 = (f32[2,3,16,128]{3,2,1,0:T(8,128)}, f32[2,3,16,128]{3,2,1,0:T(8,128)S(1)}, u32[]{:S(2)}) copy-start(f32[2,3,16,128]{3,2,1,0:T(8,128)S(1)} %get-tuple-element.18) | copy-start | bytes 147460
  38.2 21.9 %collective-permute-start.3 = (f32[91,16,128]{2,1,0:T(8,128)}, f32[91,16,128]{2,1,0:T(8,128)S(1)}, u32[]{:S(2)}, u32[]{:S(2)}) collective-permute-start(f32[91,16,128]{2,1,0:T(8,128)} %get-tuple-element.17), channel_id=1, source_target_pairs={{4,0},{8,4},{12,8},{16,12},{20,16},{24,20},{28,24},{32,28},{36,32}... | collective-permute-start | bytes 2236424 | tf_op jit(solution)/shard_map/ppermute | solution.py:478
  44.5 18.9 %collective-permute-start.2 = (f32[91,16,128]{2,1,0:T(8,128)S(1)}, f32[91,16,128]{2,1,0:T(8,128)S(1)}, u32[]{:S(2)}, u32[]{:S(2)}) collective-permute-start(f32[91,16,128]{2,1,0:T(8,128)S(1)} %get-tuple-element.15.own.own_up), channel_id=1, source_target_pairs={{0,4},{4,8},{8,12},{12,16},{16,20},{20,24},{24,28},{28,32},{32,36}... | collective-permute-start | bytes 2236424 | tf_op jit(solution)/shard_map/ppermute | solution.py:478
  46.5 12.5 %collective-permute-start.6 = (f32[128,8,128]{2,1,0:T(8,128)S(1)}, f32[128,8,128]{2,1,0:T(8,128)S(1)}, u32[]{:S(2)}, u32[]{:S(2)}) collective-permute-start(f32[128,8,128]{2,1,0:T(8,128)S(1)} %all-to-all-done), channel_id=1, source_target_pairs={{0,1},{1,0},{2,3},{3,2},{4,5},{5,4},{6,7},{7,6},{8,9},{9,8},{10,11... | collective-permute-start | bytes 1572872 | tf_op jit(solution)/shard_map/ppermute | solution.py:485
  48.4 17.2 %collective-permute-start.4 = (f32[2,3,16,128]{3,2,1,0:T(8,128)}, f32[2,3,16,128]{3,2,1,0:T(8,128)S(1)}, u32[]{:S(2)}, u32[]{:S(2)}) collective-permute-start(f32[2,3,16,128]{3,2,1,0:T(8,128)} %copy-done.7), channel_id=1, source_target_pairs={{0,8},{4,12},{8,16},{12,20},{16,24},{20,28},{24,32},{28,36},{32,40... | collective-permute-start | bytes 147464 | tf_op jit(solution)/shard_map/ppermute | solution.py:478
  50.3 15.3 %collective-permute-start.5 = (f32[2,3,16,128]{3,2,1,0:T(8,128)S(1)}, f32[2,3,16,128]{3,2,1,0:T(8,128)S(1)}, u32[]{:S(2)}, u32[]{:S(2)}) collective-permute-start(f32[2,3,16,128]{3,2,1,0:T(8,128)S(1)} %get-tuple-element.19), channel_id=1, source_target_pairs={{8,0},{12,4},{16,8},{20,12},{24,16},{28,20},{32,24},{36,28},{40,32... | collective-permute-start | bytes 147464 | tf_op jit(solution)/shard_map/ppermute | solution.py:478
